TPU v7x, 128 devices: a whole 4x4x4 slice. The times are simulated.
128 devices in a mesh: dp: 2 (over core), blk: 8 (over y_hi, x), head: 8 (over z, y_lo).
Axes of the slice: x: 4, y: 4 (y_hi: 2, y_lo: 2; y = y_hi * 2 + y_lo), z: 4, core: 2. Of those that a mesh axis runs over, the one named last changes fastest.
Arguments:
- query_input: bfloat16 [2, 12288, 3072], P('dp', ('blk', 'head')), may hold values from -6 to 6
- key_input: bfloat16 [2, 12288, 3072], P('dp', ('blk', 'head')), may hold values from -6 to 6
- value_input: bfloat16 [2, 12288, 3072], P('dp', ('blk', 'head')), may hold values from -6 to 6
- output_grad: bfloat16 [2, 12288, 3072], P('dp', ('blk', 'head')), may hold values from -16 to 16
- query_gain: float32 [3072], replicated, may hold values from 0.5 to 1.5
- key_gain: float32 [3072], replicated, may hold values from 0.5 to 1.5
- tile_lists: int32 [2, 64, 12], P('dp'), may hold values from 0 to 63, as said below
- tile_counts: int32 [2, 64], P('dp'), may hold values from 2 to 12, as said below
Outputs:
- attention: bfloat16 [2, 12288, 3072], P('dp', ('blk', 'head'))
- query_grad: bfloat16 [2, 12288, 3072], P('dp', ('blk', 'head'))
- key_grad: bfloat16 [2, 12288, 3072], P('dp', ('blk', 'head'))
- value_grad: bfloat16 [2, 12288, 3072], P('dp', ('blk', 'head'))
- query_gain_grad: float32 [3072], P(('dp', 'blk', 'head'))
- key_gain_grad: float32 [3072], P(('dp', 'blk', 'head'))
Inputs may be any that keep to these rules, and one draw needn't show every extreme that they name: `tile_lists`: tile t lies in slab t // 8, tile row (t // 4) % 2, tile column t % 4. The first tile_counts[t] entries of row t are distinct tiles, the first being t itself, each at most one slab, one tile row and one tile column away from t; the remaining entries equal t. `tile_counts`: 12 is reached in every sequence.
All inputs are finite; a program needn't handle non-finite values.
Results may differ from a plain program's by a relative error of at most 0.038.
Values may be sent and summed in bfloat16 or wider, within the bound.
A program may use at most 192 MiB of HBM per device.

v0:
```python
import jax
import jax.numpy as jnp
from jax import lax
from jax.sharding import PartitionSpec as P

HS = 128
TILE = 192
KMAX = 12


EPSILON = 1e-06


def extended(x, sides, width):
    for axis, dim in sides:
        peers, length = (lax.axis_size(axis), x.shape[dim])
        up = [(i, (i + 1) % peers) for i in range(peers - 1)]
        down = [(j, i) for i, j in up]
        last = lax.slice_in_dim(x, length - width, length, axis=dim)
        first = lax.slice_in_dim(x, 0, width, axis=dim)
        before = lax.ppermute(last, axis, up)
        after = lax.ppermute(first, axis, down)
        x = jnp.concatenate([before, x, after], axis=dim)
    return x


def from_behind(x, axis, by):
    peers = lax.axis_size(axis)
    pairs = [(i, i + by) for i in range(peers) if 0 <= i + by < peers]
    return lax.ppermute(x, axis, pairs)


def normalize(raw_input, gain_vec):
    widened = raw_input.astype(jnp.float32)
    factor = lax.rsqrt(jnp.mean(widened * widened, axis=-1, keepdims=True) + EPSILON)
    normed = widened * factor
    return (normed, factor, (normed * gain_vec).astype(jnp.bfloat16))


def norm_back(grad_input, normed, factor, gain_vec):
    grad_wide = grad_input.astype(jnp.float32)
    scaled = grad_wide * gain_vec
    inner = jnp.mean(scaled * normed, axis=-1, keepdims=True)
    return (
        (factor * (scaled - normed * inner)).astype(jnp.bfloat16),
        jnp.sum(grad_wide * normed, axis=0),
    )


def head_major(tokens_rows, heads_here):
    return tokens_rows.reshape(tokens_rows.shape[0], heads_here, HS).transpose(1, 0, 2)


def tile_step(query_tile, grad_tile, key_block, value_block, live_count):
    score_scale = HS ** (-0.5)
    scores = (
        jnp.einsum("hqd,hkd->hqk", query_tile, key_block, preferred_element_type=jnp.float32)
        * score_scale
    )
    slot_of = jnp.arange(key_block.shape[1], dtype=jnp.int32) // TILE
    live_slots = (slot_of < live_count)[None, None, :]
    scores = jnp.where(live_slots, scores, -jnp.inf)
    row_max = jnp.max(scores, axis=2, keepdims=True)
    exponent = jnp.exp(scores - row_max)
    weights = (exponent / jnp.sum(exponent, axis=2, keepdims=True)).astype(jnp.bfloat16)
    output = jnp.einsum(
        "hqk,hkd->hqd", weights, value_block, preferred_element_type=jnp.float32
    ).astype(jnp.bfloat16)
    grad_probs = jnp.einsum(
        "hqd,hkd->hqk", grad_tile, value_block, preferred_element_type=jnp.float32
    )
    weights_wide = weights.astype(jnp.float32)
    row_delta = jnp.sum(weights_wide * grad_probs, axis=2, keepdims=True)
    grad_scores = (weights_wide * (grad_probs - row_delta)).astype(jnp.bfloat16)
    query_att = (
        score_scale
        * jnp.einsum("hqk,hkd->hqd", grad_scores, key_block, preferred_element_type=jnp.float32)
    ).astype(jnp.bfloat16)
    key_part = score_scale * jnp.einsum(
        "hqk,hqd->hkd", grad_scores, query_tile, preferred_element_type=jnp.float32
    )
    value_part = jnp.einsum("hqk,hqd->hkd", weights, grad_tile, preferred_element_type=jnp.float32)
    return (output, query_att, key_part, value_part)


def shards(
    query_input, key_input, value_input, output_grad, query_gain, key_gain, tile_lists, tile_counts
):
    q_hat, q_factor, queries = normalize(query_input[0], query_gain)
    k_hat, k_factor, keys = normalize(key_input[0], key_gain)
    query_heads, key_heads, value_heads, grad_heads = (
        lax.all_to_all(queries, "head", split_axis=1, concat_axis=0, tiled=True),
        lax.all_to_all(keys, "head", split_axis=1, concat_axis=0, tiled=True),
        lax.all_to_all(value_input[0], "head", split_axis=1, concat_axis=0, tiled=True),
        lax.all_to_all(output_grad[0], "head", split_axis=1, concat_axis=0, tiled=True),
    )
    slab_tokens = query_heads.shape[0]
    head_width = query_heads.shape[1]
    per_slab = slab_tokens // TILE
    heads_here = head_width // HS
    slab_index = lax.axis_index("blk")
    lists_here = lax.dynamic_slice_in_dim(tile_lists[0], slab_index * per_slab, per_slab, 0)
    counts_here = lax.dynamic_slice_in_dim(tile_counts[0], slab_index * per_slab, per_slab, 0)
    relative = lists_here - (slab_index - 1) * per_slab
    query_major = head_major(query_heads, heads_here)
    grad_major = head_major(grad_heads, heads_here)
    stacked = jnp.stack([head_major(key_heads, heads_here), head_major(value_heads, heads_here)])
    padded = extended(stacked, (("blk", 2),), slab_tokens)
    padded_grid = padded.reshape(2, heads_here, 3 * per_slab, TILE, HS)
    span = KMAX * TILE

    def visit(totals, inputs):
        tile_number, live_count, targets = inputs
        query_tile = lax.dynamic_slice_in_dim(query_major, tile_number * TILE, TILE, 1)
        grad_tile = lax.dynamic_slice_in_dim(grad_major, tile_number * TILE, TILE, 1)
        chosen = jnp.take(padded_grid, targets, axis=2).reshape(2, heads_here, span, HS)
        tile_out, tile_qgrad, key_part, value_part = tile_step(
            query_tile, grad_tile, chosen[0], chosen[1], live_count
        )
        totals = totals.at[0, :, targets].add(
            key_part.reshape(heads_here, KMAX, TILE, HS).transpose(1, 0, 2, 3)
        )
        totals = totals.at[1, :, targets].add(
            value_part.reshape(heads_here, KMAX, TILE, HS).transpose(1, 0, 2, 3)
        )
        return (totals, (tile_out, tile_qgrad))

    start_totals = jnp.zeros((2, heads_here, 3 * per_slab, TILE, HS), jnp.float32)
    totals, tile_outs = lax.scan(
        visit, start_totals, (jnp.arange(per_slab, dtype=jnp.int32), counts_here, relative)
    )
    from_upper = from_behind(totals[:, :, :per_slab], "blk", -1)
    from_lower = from_behind(totals[:, :, 2 * per_slab :], "blk", 1)
    own_grads = (totals[:, :, per_slab : 2 * per_slab] + from_upper + from_lower).astype(
        jnp.bfloat16
    )
    own_grads = (
        own_grads.reshape(2, heads_here, slab_tokens, HS)
        .transpose(0, 2, 1, 3)
        .reshape(2, slab_tokens, head_width)
    )
    attention_heads = tile_outs[0].transpose(0, 2, 1, 3).reshape(slab_tokens, head_width)
    query_att_heads = tile_outs[1].transpose(0, 2, 1, 3).reshape(slab_tokens, head_width)
    attention, query_att, key_att, value_grad = (
        lax.all_to_all(attention_heads, "head", split_axis=0, concat_axis=1, tiled=True),
        lax.all_to_all(query_att_heads, "head", split_axis=0, concat_axis=1, tiled=True),
        lax.all_to_all(own_grads[0], "head", split_axis=0, concat_axis=1, tiled=True),
        lax.all_to_all(own_grads[1], "head", split_axis=0, concat_axis=1, tiled=True),
    )
    query_grad, query_gain_part = norm_back(query_att, q_hat, q_factor, query_gain)
    key_grad, key_gain_part = norm_back(key_att, k_hat, k_factor, key_gain)
    query_gain_grad, key_gain_grad = (
        lax.psum_scatter(query_gain_part, ("dp", "blk", "head"), scatter_dimension=0, tiled=True),
        lax.psum_scatter(key_gain_part, ("dp", "blk", "head"), scatter_dimension=0, tiled=True),
    )
    return (
        attention[None],
        query_grad[None],
        key_grad[None],
        value_grad[None],
        query_gain_grad,
        key_gain_grad,
    )


def solution(mesh):
    placed = (
        P("dp", ("blk", "head"), None),
        P("dp", ("blk", "head"), None),
        P("dp", ("blk", "head"), None),
        P("dp", ("blk", "head"), None),
        P(),
        P(),
        P("dp", None, None),
        P("dp", None),
    )
    return jax.shard_map(
        shards,
        mesh=mesh,
        in_specs=placed,
        out_specs=(
            P("dp", ("blk", "head"), None),
            P("dp", ("blk", "head"), None),
            P("dp", ("blk", "head"), None),
            P("dp", ("blk", "head"), None),
            P(("dp", "blk", "head")),
            P(("dp", "blk", "head")),
        ),
        check_vma=False,
    )
```

profile of v0, /device:TPU:1, one launch (start us, length us, event | category | flops | bytes accessed | tf_op | source)
XLA Modules:
  0.0 812.3 jit_solution(2475681951949318416)
XLA Ops:
  13.1 13.3 %all-to-all-done.2 = bf16[192,8,384]{2,0,1:T(8,128)(2,1)S(1)} async-done(((bf16[192,8,384]{2,0,1:T(8,128)(2,1)}), bf16[192,8,384]{2,0,1:T(8,128)(2,1)S(1)}, u32[]{:S(2)}, u32[]{:S(2)}) %all-to-all-start.2) | async-done | bytes 1179680 | tf_op jit(solution)/shard_map/all_to_all | solution.py:94
  31.7 13.8 %all-to-all-done.1 = bf16[192,8,384]{2,0,1:T(8,128)(2,1)S(1)} async-done(((bf16[192,8,384]{2,0,1:T(8,128)(2,1)}), bf16[192,8,384]{2,0,1:T(8,128)(2,1)S(1)}, u32[]{:S(2)}, u32[]{:S(2)}) %all-to-all-start.1) | async-done | bytes 1179680 | tf_op jit(solution)/shard_map/all_to_all | solution.py:93
  87.0 61.8 %all-to-all-done = bf16[192,8,384]{2,0,1:T(8,128)(2,1)S(1)} async-done(((bf16[192,8,384]{2,0,1:T(8,128)(2,1)}), bf16[192,8,384]{2,0,1:T(8,128)(2,1)S(1)}, u32[]{:S(2)}, u32[]{:S(2)}) %all-to-all-start) | async-done | bytes 1179680 | tf_op jit(solution)/shard_map/all_to_all | solution.py:92
  161.2 10.3 %copy.86 = bf16[2,3,4608,128]{3,2,1,0:T(8,128)(2,1)} copy(bf16[2,3,4608,128]{2,3,1,0:T(8,128)(2,1)} %pad_maximum_fusion) | data formatting | bytes 14155776 | tf_op jit(solution)/shard_map/concatenate | solution.py:23
  178.8 375.8 %while.16 = (s32[]{:T(128)}, f32[2,3,24,192,128]{4,3,2,1,0:T(8,128)}, bf16[8,3,192,128]{3,2,1,0:T(8,128)(2,1)}, bf16[8,3,192,128]{3,2,1,0:T(8,128)(2,1)}, s32[8,...) while((s32[]{:T(128)}, ...), condition=%wide.region_8.9_spmd, body=%wide.region_2.8_spmd.sunk | while | flops 2060352640 | bytes 118576832 | solution.py:129
  208.0 8.5 %scatter_fusion = f32[2,3,24,192,128]{4,3,2,1,0:T(8,128)} fusion(f32[2,3,24,192,128]{4,3,2,1,0:T(8,128)} %get-tuple-element.312, s32[12]{0:T(128)S(1)} %select_bitcast_fusion.7, f32[12,3,192,128]{3,2,1,0:T(8,128)S(1)} %bitcast.171), kind=kCustom, calls=%fused_computation.1.clone.1 | custom fusion | flops 884736 | bytes 10616928 | tf_op jit(solution)/shard_map/while/body/eval_jaxpr/scatter-add | solution.py:120
  216.5 9.7 %scatter_fusion.1 = f32[2,3,24,192,128]{4,3,2,1,0:T(8,128)} fusion(f32[2,3,24,192,128]{4,3,2,1,0:T(8,128)} %scatter_fusion, s32[12]{0:T(128)S(1)} %get-tuple-element.296, f32[12,3,192,128]{3,2,1,0:T(8,128)} %bitcast.172), kind=kCustom, calls=%fused_computation.2.clone.1 | custom fusion | flops 884736 | bytes 10616928 | tf_op jit(solution)/shard_map/while/body/eval_jaxpr/scatter-add | solution.py:123
  255.2 8.4 %scatter_fusion = f32[2,3,24,192,128]{4,3,2,1,0:T(8,128)} fusion(f32[2,3,24,192,128]{4,3,2,1,0:T(8,128)} %get-tuple-element.312, s32[12]{0:T(128)S(1)} %select_bitcast_fusion.7, f32[12,3,192,128]{3,2,1,0:T(8,128)S(1)} %bitcast.171), kind=kCustom, calls=%fused_computation.1.clone.1 | custom fusion | flops 884736 | bytes 10616928 | tf_op jit(solution)/shard_map/while/body/eval_jaxpr/scatter-add | solution.py:120
  263.6 9.2 %scatter_fusion.1 = f32[2,3,24,192,128]{4,3,2,1,0:T(8,128)} fusion(f32[2,3,24,192,128]{4,3,2,1,0:T(8,128)} %scatter_fusion, s32[12]{0:T(128)S(1)} %get-tuple-element.296, f32[12,3,192,128]{3,2,1,0:T(8,128)} %bitcast.172), kind=kCustom, calls=%fused_computation.2.clone.1 | custom fusion | flops 884736 | bytes 10616928 | tf_op jit(solution)/shard_map/while/body/eval_jaxpr/scatter-add | solution.py:123
  301.9 8.4 %scatter_fusion = f32[2,3,24,192,128]{4,3,2,1,0:T(8,128)} fusion(f32[2,3,24,192,128]{4,3,2,1,0:T(8,128)} %get-tuple-element.312, s32[12]{0:T(128)S(1)} %select_bitcast_fusion.7, f32[12,3,192,128]{3,2,1,0:T(8,128)S(1)} %bitcast.171), kind=kCustom, calls=%fused_computation.1.clone.1 | custom fusion | flops 884736 | bytes 10616928 | tf_op jit(solution)/shard_map/while/body/eval_jaxpr/scatter-add | solution.py:120
  310.3 9.4 %scatter_fusion.1 = f32[2,3,24,192,128]{4,3,2,1,0:T(8,128)} fusion(f32[2,3,24,192,128]{4,3,2,1,0:T(8,128)} %scatter_fusion, s32[12]{0:T(128)S(1)} %get-tuple-element.296, f32[12,3,192,128]{3,2,1,0:T(8,128)} %bitcast.172), kind=kCustom, calls=%fused_computation.2.clone.1 | custom fusion | flops 884736 | bytes 10616928 | tf_op jit(solution)/shard_map/while/body/eval_jaxpr/scatter-add | solution.py:123
  348.7 8.5 %scatter_fusion = f32[2,3,24,192,128]{4,3,2,1,0:T(8,128)} fusion(f32[2,3,24,192,128]{4,3,2,1,0:T(8,128)} %get-tuple-element.312, s32[12]{0:T(128)S(1)} %select_bitcast_fusion.7, f32[12,3,192,128]{3,2,1,0:T(8,128)S(1)} %bitcast.171), kind=kCustom, calls=%fused_computation.1.clone.1 | custom fusion | flops 884736 | bytes 10616928 | tf_op jit(solution)/shard_map/while/body/eval_jaxpr/scatter-add | solution.py:120
  357.2 9.6 %scatter_fusion.1 = f32[2,3,24,192,128]{4,3,2,1,0:T(8,128)} fusion(f32[2,3,24,192,128]{4,3,2,1,0:T(8,128)} %scatter_fusion, s32[12]{0:T(128)S(1)} %get-tuple-element.296, f32[12,3,192,128]{3,2,1,0:T(8,128)} %bitcast.172), kind=kCustom, calls=%fused_computation.2.clone.1 | custom fusion | flops 884736 | bytes 10616928 | tf_op jit(solution)/shard_map/while/body/eval_jaxpr/scatter-add | solution.py:123
  395.8 8.4 %scatter_fusion = f32[2,3,24,192,128]{4,3,2,1,0:T(8,128)} fusion(f32[2,3,24,192,128]{4,3,2,1,0:T(8,128)} %get-tuple-element.312, s32[12]{0:T(128)S(1)} %select_bitcast_fusion.7, f32[12,3,192,128]{3,2,1,0:T(8,128)S(1)} %bitcast.171), kind=kCustom, calls=%fused_computation.1.clone.1 | custom fusion | flops 884736 | bytes 10616928 | tf_op jit(solution)/shard_map/while/body/eval_jaxpr/scatter-add | solution.py:120
  404.2 9.4 %scatter_fusion.1 = f32[2,3,24,192,128]{4,3,2,1,0:T(8,128)} fusion(f32[2,3,24,192,128]{4,3,2,1,0:T(8,128)} %scatter_fusion, s32[12]{0:T(128)S(1)} %get-tuple-element.296, f32[12,3,192,128]{3,2,1,0:T(8,128)} %bitcast.172), kind=kCustom, calls=%fused_computation.2.clone.1 | custom fusion | flops 884736 | bytes 10616928 | tf_op jit(solution)/shard_map/while/body/eval_jaxpr/scatter-add | solution.py:123
  442.6 8.5 %scatter_fusion = f32[2,3,24,192,128]{4,3,2,1,0:T(8,128)} fusion(f32[2,3,24,192,128]{4,3,2,1,0:T(8,128)} %get-tuple-element.312, s32[12]{0:T(128)S(1)} %select_bitcast_fusion.7, f32[12,3,192,128]{3,2,1,0:T(8,128)S(1)} %bitcast.171), kind=kCustom, calls=%fused_computation.1.clone.1 | custom fusion | flops 884736 | bytes 10616928 | tf_op jit(solution)/shard_map/while/body/eval_jaxpr/scatter-add | solution.py:120
  451.0 9.6 %scatter_fusion.1 = f32[2,3,24,192,128]{4,3,2,1,0:T(8,128)} fusion(f32[2,3,24,192,128]{4,3,2,1,0:T(8,128)} %scatter_fusion, s32[12]{0:T(128)S(1)} %get-tuple-element.296, f32[12,3,192,128]{3,2,1,0:T(8,128)} %bitcast.172), kind=kCustom, calls=%fused_computation.2.clone.1 | custom fusion | flops 884736 | bytes 10616928 | tf_op jit(solution)/shard_map/while/body/eval_jaxpr/scatter-add | solution.py:123
  489.7 8.3 %scatter_fusion = f32[2,3,24,192,128]{4,3,2,1,0:T(8,128)} fusion(f32[2,3,24,192,128]{4,3,2,1,0:T(8,128)} %get-tuple-element.312, s32[12]{0:T(128)S(1)} %select_bitcast_fusion.7, f32[12,3,192,128]{3,2,1,0:T(8,128)S(1)} %bitcast.171), kind=kCustom, calls=%fused_computation.1.clone.1 | custom fusion | flops 884736 | bytes 10616928 | tf_op jit(solution)/shard_map/while/body/eval_jaxpr/scatter-add | solution.py:120
  498.0 9.4 %scatter_fusion.1 = f32[2,3,24,192,128]{4,3,2,1,0:T(8,128)} fusion(f32[2,3,24,192,128]{4,3,2,1,0:T(8,128)} %scatter_fusion, s32[12]{0:T(128)S(1)} %get-tuple-element.296, f32[12,3,192,128]{3,2,1,0:T(8,128)} %bitcast.172), kind=kCustom, calls=%fused_computation.2.clone.1 | custom fusion | flops 884736 | bytes 10616928 | tf_op jit(solution)/shard_map/while/body/eval_jaxpr/scatter-add | solution.py:123
  536.4 8.5 %scatter_fusion = f32[2,3,24,192,128]{4,3,2,1,0:T(8,128)} fusion(f32[2,3,24,192,128]{4,3,2,1,0:T(8,128)} %get-tuple-element.312, s32[12]{0:T(128)S(1)} %select_bitcast_fusion.7, f32[12,3,192,128]{3,2,1,0:T(8,128)S(1)} %bitcast.171), kind=kCustom, calls=%fused_computation.1.clone.1 | custom fusion | flops 884736 | bytes 10616928 | tf_op jit(solution)/shard_map/while/body/eval_jaxpr/scatter-add | solution.py:120
  544.9 9.5 %scatter_fusion.1 = f32[2,3,24,192,128]{4,3,2,1,0:T(8,128)} fusion(f32[2,3,24,192,128]{4,3,2,1,0:T(8,128)} %scatter_fusion, s32[12]{0:T(128)S(1)} %get-tuple-element.296, f32[12,3,192,128]{3,2,1,0:T(8,128)} %bitcast.172), kind=kCustom, calls=%fused_computation.2.clone.1 | custom fusion | flops 884736 | bytes 10616928 | tf_op jit(solution)/shard_map/while/body/eval_jaxpr/scatter-add | solution.py:123
  554.7 8.6 %fusion.37 = (f32[2,3,8,192,128]{4,3,2,1,0:T(8,128)}, f32[2,3,8,192,128]{4,3,2,1,0:T(8,128)}) fusion(f32[2,3,24,192,128]{4,3,2,1,0:T(8,128)} %get-tuple-element.136), kind=kLoop, calls=%fused_computation.85 | loop fusion | bytes 18874368 | tf_op jit(solution)/shard_map/slice | solution.py:132
  576.6 90.2 %all-to-all-done.5 = bf16[8,192,384]{2,1,0:T(8,128)(2,1)S(1)} async-done(((bf16[8,192,384]{2,1,0:T(8,128)(2,1)}), bf16[8,192,384]{2,1,0:T(8,128)(2,1)S(1)}, u32[]{:S(2)}, u32[]{:S(2)}) %all-to-all-start.5) | async-done | bytes 1179680 | tf_op jit(solution)/shard_map/all_to_all | solution.py:146
  736.5 65.8 %all-reduce.4 = (f32[3072]{0:T(1024)S(1)}, f32[3072]{0:T(1024)S(1)}) all-reduce(f32[3072]{0:T(1024)S(1)} %copy-done.23, f32[3072]{0:T(1024)S(1)} %reduce_sum.89), channel_id=2, replica_groups=mesh['dp'=2,'blk'=8,'head'=8] {'dp','blk','head'}, use_global_device_ids=true, to_apply=%region_12.13.clone | all-reduce | flops 6144 | bytes 49152
  (370 shorter events, 397.4 us)
Async XLA Ops:
  0.6 82.9 %copy-start = (s32[1,64,12]{1,0,2:T(1,128)S(1)}, s32[1,64,12]{1,0,2:T(1,128)}, u32[]{:S(2)}) copy-start(s32[1,64,12]{1,0,2:T(1,128)} %param.16) | copy-start | bytes 9220
  3.3 23.1 %all-to-all-start.2 = ((bf16[192,8,384]{2,0,1:T(8,128)(2,1)}), bf16[192,8,384]{2,0,1:T(8,128)(2,1)S(1)}, u32[]{:S(2)}, u32[]{:S(2)}) async-start(bf16[192,8,384]{2,0,1:T(8,128)(2,1)} %copy.84), calls=%async_computation.2 | async-start | bytes 2359296 | tf_op jit(solution)/shard_map/all_to_all | solution.py:94
  12.0 18.3 %copy-start.15 = (bf16[1,192,3072]{2,1,0:T(8,128)(2,1)S(1)}, bf16[1,192,3072]{2,1,0:T(8,128)(2,1)}, u32[]{:S(2)}) copy-start(bf16[1,192,3072]{2,1,0:T(8,128)(2,1)} %param.13) | copy-start | bytes 3538948
  26.5 19.0 %all-to-all-start.1 = ((bf16[192,8,384]{2,0,1:T(8,128)(2,1)}), bf16[192,8,384]{2,0,1:T(8,128)(2,1)S(1)}, u32[]{:S(2)}, u32[]{:S(2)}) async-start(bf16[192,8,384]{2,0,1:T(8,128)(2,1)} %copy.82), calls=%async_computation.1 | async-start | bytes 2359296 | tf_op jit(solution)/shard_map/all_to_all | solution.py:93
  30.5 19.4 %copy-start.20 = (f32[3072]{0:T(1024)S(1)}, f32[3072]{0:T(1024)}, u32[]{:S(2)}) copy-start(f32[3072]{0:T(1024)} %param.14) | copy-start | bytes 36868
  30.5 20.0 %copy-start.6 = (bf16[1,192,3072]{2,1,0:T(8,128)(2,1)S(1)}, bf16[1,192,3072]{2,1,0:T(8,128)(2,1)}, u32[]{:S(2)}) copy-start(bf16[1,192,3072]{2,1,0:T(8,128)(2,1)} %param.10) | copy-start | bytes 3538948
  45.5 32.8 %all-to-all-start.3 = ((bf16[192,8,384]{2,0,1:T(8,128)(2,1)}), bf16[192,8,384]{2,0,1:T(8,128)(2,1)}, u32[]{:S(2)}, u32[]{:S(2)}) async-start(bf16[192,8,384]{2,0,1:T(8,128)(2,1)} %copy.87), calls=%async_computation.3 | async-start | bytes 2359296 | tf_op jit(solution)/shard_map/all_to_all | solution.py:95
  50.7 25.9 %copy-start.4 = (f32[24,8,8,384]{3,2,1,0:T(8,128)}, f32[24,8,8,384]{3,2,1,0:T(8,128)S(1)}, u32[]{:S(2)}) copy-start(f32[24,8,8,384]{3,2,1,0:T(8,128)S(1)} %copy.109) | copy-start | bytes 7077892
  66.3 10.3 %copy-start.19 = (f32[8,384]{1,0:T(8,128)S(1)}, f32[8,384]{1,0:T(8,128)}, u32[]{:S(2)}) copy-start(f32[8,384]{1,0:T(8,128)} %mul.198) | copy-start | bytes 36868
  69.6 85.3 %collective-permute-start.1 = (bf16[2,3,1536,128]{2,3,1,0:T(8,128)(2,1)}, bf16[2,3,1536,128]{2,3,1,0:T(8,128)(2,1)}, u32[]{:S(2)}, u32[]{:S(2)}) collective-permute-start(bf16[2,3,1536,128]{2,3,1,0:T(8,128)(2,1)} %pad_maximum_fusion.1), channel_id=1, source_target_pairs={{8,0},{16,8},{24,16},{32,24},{40,32},{48,40},{56,48},{9,1},{17,9},... | collective-permute-start | bytes 7077896 | tf_op jit(solution)/shard_map/ppermute | solution.py:22
  70.9 84.0 %collective-permute-start = (bf16[2,3,1536,128]{2,3,1,0:T(8,128)(2,1)}, bf16[2,3,1536,128]{2,3,1,0:T(8,128)(2,1)}, u32[]{:S(2)}, u32[]{:S(2)}) collective-permute-start(bf16[2,3,1536,128]{2,3,1,0:T(8,128)(2,1)} %pad_maximum_fusion.1), channel_id=1, source_target_pairs={{0,8},{8,16},{16,24},{24,32},{32,40},{40,48},{48,56},{1,9},{9,17},... | collective-permute-start | bytes 7077896 | tf_op jit(solution)/shard_map/ppermute | solution.py:21
  78.3 70.5 %all-to-all-start = ((bf16[192,8,384]{2,0,1:T(8,128)(2,1)}), bf16[192,8,384]{2,0,1:T(8,128)(2,1)S(1)}, u32[]{:S(2)}, u32[]{:S(2)}) async-start(bf16[192,8,384]{2,0,1:T(8,128)(2,1)} %copy.80), calls=%async_computation | async-start | bytes 2359296 | tf_op jit(solution)/shard_map/all_to_all | solution.py:92
  216.5 9.7 %copy-start.29 = (s32[8,12]{1,0:T(8,128)S(1)}, s32[8,12]{1,0:T(8,128)}, u32[]{:S(2)}) copy-start(s32[8,12]{1,0:T(8,128)} %copy-done.28) | copy-start | bytes 1156 | tf_op jit(solution)/shard_map/while
  216.5 9.7 %copy-start.32 = (s32[8]{0:T(128)S(1)}, s32[8]{0:T(128)}, u32[]{:S(2)}) copy-start(s32[8]{0:T(128)} %copy-done.31) | copy-start | bytes 100 | tf_op jit(solution)/shard_map/while
  357.2 9.6 %copy-start.32 = (s32[8]{0:T(128)S(1)}, s32[8]{0:T(128)}, u32[]{:S(2)}) copy-start(s32[8]{0:T(128)} %copy-done.31) | copy-start | bytes 100 | tf_op jit(solution)/shard_map/while
  451.0 9.6 %copy-start.29 = (s32[8,12]{1,0:T(8,128)S(1)}, s32[8,12]{1,0:T(8,128)}, u32[]{:S(2)}) copy-start(s32[8,12]{1,0:T(8,128)} %copy-done.28) | copy-start | bytes 1156 | tf_op jit(solution)/shard_map/while
  451.0 9.6 %copy-start.32 = (s32[8]{0:T(128)S(1)}, s32[8]{0:T(128)}, u32[]{:S(2)}) copy-start(s32[8]{0:T(128)} %copy-done.31) | copy-start | bytes 100 | tf_op jit(solution)/shard_map/while
  554.7 16.0 %copy-start.16 = (bf16[8,3,192,128]{3,2,1,0:T(8,128)(2,1)S(1)}, bf16[8,3,192,128]{3,2,1,0:T(8,128)(2,1)}, u32[]{:S(2)}) copy-start(bf16[8,3,192,128]{3,2,1,0:T(8,128)(2,1)} %get-tuple-element.135) | copy-start | bytes 3538948
  563.2 107.8 %collective-permute-start.2 = (f32[2,3,8,192,128]{4,3,2,1,0:T(8,128)}, f32[2,3,8,192,128]{4,3,2,1,0:T(8,128)}, u32[]{:S(2)}, u32[]{:S(2)}) collective-permute-start(f32[2,3,8,192,128]{4,3,2,1,0:T(8,128)} %get-tuple-element.212), channel_id=1, source_target_pairs={{8,0},{16,8},{24,16},{32,24},{40,32},{48,40},{56,48},{9,1},{17,9},... | collective-permute-start | bytes 14155784 | tf_op jit(solution)/shard_map/ppermute | solution.py:30
  564.5 106.5 %collective-permute-start.3 = (f32[2,3,8,192,128]{4,3,2,1,0:T(8,128)}, f32[2,3,8,192,128]{4,3,2,1,0:T(8,128)}, u32[]{:S(2)}, u32[]{:S(2)}) collective-permute-start(f32[2,3,8,192,128]{4,3,2,1,0:T(8,128)} %get-tuple-element.213), channel_id=1, source_target_pairs={{0,8},{8,16},{16,24},{24,32},{32,40},{40,48},{48,56},{1,9},{9,17},... | collective-permute-start | bytes 14155784 | tf_op jit(solution)/shard_map/ppermute | solution.py:30
  571.8 94.9 %all-to-all-start.5 = ((bf16[8,192,384]{2,1,0:T(8,128)(2,1)}), bf16[8,192,384]{2,1,0:T(8,128)(2,1)S(1)}, u32[]{:S(2)}, u32[]{:S(2)}) async-start(bf16[8,192,384]{2,1,0:T(8,128)(2,1)} %copy_bitcast_fusion.2), calls=%async_computation.5 | async-start | bytes 2359296 | tf_op jit(solution)/shard_map/all_to_all | solution.py:146
  666.7 23.3 %all-to-all-start.4 = ((bf16[8,192,384]{2,1,0:T(8,128)(2,1)}), bf16[8,192,384]{2,1,0:T(8,128)(2,1)}, u32[]{:S(2)}, u32[]{:S(2)}) async-start(bf16[8,192,384]{2,1,0:T(8,128)(2,1)} %copy_bitcast_fusion.3), calls=%async_computation.4 | async-start | bytes 2359296 | tf_op jit(solution)/shard_map/all_to_all | solution.py:145
  690.1 21.0 %all-to-all-start.7 = ((bf16[8,192,384]{2,1,0:T(8,128)(2,1)}), bf16[8,192,384]{2,1,0:T(8,128)(2,1)}, u32[]{:S(2)}, u32[]{:S(2)}) async-start(bf16[8,192,384]{2,1,0:T(8,128)(2,1)} %copy.98), calls=%async_computation.7 | async-start | bytes 2359296 | tf_op jit(solution)/shard_map/all_to_all | solution.py:148
  711.1 21.7 %all-to-all-start.6 = ((bf16[8,192,384]{2,1,0:T(8,128)(2,1)}), bf16[8,192,384]{2,1,0:T(8,128)(2,1)}, u32[]{:S(2)}, u32[]{:S(2)}) async-start(bf16[8,192,384]{2,1,0:T(8,128)(2,1)} %copy.96), calls=%async_computation.6 | async-start | bytes 2359296 | tf_op jit(solution)/shard_map/all_to_all | solution.py:147
  (49 other events, 246.0 us)
where the time goes:
time: 822 us; the launch traced here: 812 us
  other arithmetic  202 us (25%)
  waiting for transfers between devices  187 us (23%)
  local copies, waits for them, and re-layouts  167 us (20%)
  matrix products  130 us (16%)
  blocking collectives  65.8 us (8%)
  starting transfers between devices  51.6 us (6%)
    all_to_all x1, waiting for transfers between devices, shards(): lax.all_to_all(query_att_heads, 'head', split_axis=0, concat_axis=1, tile...  90.2 us
    scatter-add x8, other arithmetic, visit(): totals.at[1, :, targets]  75.7 us
    scatter-add x8, other arithmetic, visit(): totals.at[0, :, targets]  67.4 us
    unnamed x1, blocking collectives  65.8 us
    all_to_all x1, waiting for transfers between devices, shards(): lax.all_to_all(queries, 'head', split_axis=1, concat_axis=0, tiled=True)  61.8 us
    sub x8, matrix products, tile_step(): exponent = jnp.exp(scores - row_max)  39.5 us
    gather x8, local copies, waits for them, and re-layouts, visit(): jnp.take(padded_grid, targets, axis=2).reshape(2, heads_here, span, HS)  33.9 us
    dot_general x8, matrix products, tile_step(): jnp.einsum('hqd,hkd->hqk', grad_tile, value_block, preferred_element_type...  30.1 us
  transfers between devices with their start and end apart: 12, of which 5 were waited for; matrix products, arithmetic and copies ran while one was open for 9% of the time, Pallas kernels for 0%

commit v1 on v0

v1 whole, which is shorter than its diff:
```python
import functools

import jax
import jax.numpy as jnp
from jax import lax
from jax.experimental import pallas as pl
from jax.experimental.pallas import tpu as pltpu
from jax.sharding import PartitionSpec as P

HS = 128
TILE = 192
KMAX = 12
HEADS = 24
HPD = 3
COLS = 4
NB = 8
NH = 8
F = HEADS * HS
CH = 2 * TILE
ROWS = 16
EPSILON = 1e-06
SCALE = HS**-0.5
SCALE2 = SCALE * 1.4426950408889634
FAR = -1e30
f32 = jnp.float32
bf16 = jnp.bfloat16


def nn(a, b):
    return lax.dot_general(a, b, (((1,), (0,)), ((), ())), preferred_element_type=f32)


def nt(a, b):
    return lax.dot_general(a, b, (((1,), (1,)), ((), ())), preferred_element_type=f32)


def wait_for(ref, sem):
    pltpu.make_async_copy(ref, ref, sem).wait()


def kernel(
    q_in,
    k_in,
    v_in,
    g_in,
    q_gain,
    k_gain,
    bias,
    att_out,
    qgrad_out,
    kgrad_out,
    vgrad_out,
    gain_out,
    q_stage,
    k_stage,
    q_fac,
    k_fac,
    qbuf,
    gbuf,
    kbuf,
    vbuf,
    kt_buf,
    vt_buf,
    s_buf,
    p_buf,
    acc_k,
    acc_v,
    own_acc,
    edge_send,
    edge_recv,
    own_send,
    o_send,
    dq_send,
    dq_recv,
    dk_recv,
    gain_acc,
    in_send,
    in_recv,
    halo_send,
    halo_recv,
    edge_ssem,
    edge_rsem,
    back_send,
    back_recv,
):
    b = lax.axis_index("blk")
    g = lax.axis_index("head")
    has_low = b > 0
    has_high = b < NB - 1
    my_row = g // COLS
    my_col = g % COLS
    my_rows = pl.ds(pl.multiple_of(my_row * TILE, TILE), TILE)

    barrier = pltpu.get_barrier_semaphore()

    def greet(i, carry):
        pl.semaphore_signal(barrier, inc=1, device_id={"head": (g + i) % NH})
        return carry

    lax.fori_loop(1, NH, greet, 0)

    @pl.when(has_low)
    def _():
        pl.semaphore_signal(barrier, inc=1, device_id={"blk": b - 1})

    @pl.when(has_high)
    def _():
        pl.semaphore_signal(barrier, inc=1, device_id={"blk": b + 1})

    def clear_side(slab, side):
        zeros = jnp.zeros((CH, HS), bf16)

        def one(e, carry):
            h, c = e // COLS, e % COLS
            kbuf[h, c, slab] = zeros
            vbuf[h, c, slab] = zeros
            edge_recv[e, side, 0] = zeros
            edge_recv[e, side, 1] = zeros
            return carry

        lax.fori_loop(0, HPD * COLS, one, 0)

    @pl.when(jnp.logical_not(has_low))
    def _():
        clear_side(0, 0)

    @pl.when(jnp.logical_not(has_high))
    def _():
        clear_side(2, 1)

    def normalize(x_in, gain, stage, fac):
        def block(i, carry):
            rows = pl.ds(pl.multiple_of(i * ROWS, ROWS), ROWS)
            total = jnp.zeros((ROWS, HS), f32)
            for h in range(HEADS):
                x = x_in[rows, h * HS : (h + 1) * HS].astype(f32)
                total = total + x * x
            mean = jnp.sum(total, axis=1, keepdims=True) * (1.0 / F)
            factor = jnp.broadcast_to(lax.rsqrt(mean + EPSILON), (ROWS, HS))
            fac[rows, :] = factor
            for h in range(HEADS):
                x = x_in[rows, h * HS : (h + 1) * HS].astype(f32)
                stage[h, rows, :] = (x * factor * gain[:, h * HS : (h + 1) * HS]).astype(bf16)
            return carry

        lax.fori_loop(0, TILE // ROWS, block, 0)

    def send_in(h, which, src_of, dst):
        here = pltpu.make_async_copy(src_of(g * HPD + h), dst, in_recv.at[which, h])
        here.start()

        def one(i, carry):
            to = (g + i) % NH
            pltpu.make_async_remote_copy(
                src_ref=src_of(to * HPD + h),
                dst_ref=dst,
                send_sem=in_send.at[which],
                recv_sem=in_recv.at[which, h],
                device_id={"head": to},
            ).start()
            return carry

        lax.fori_loop(1, NH, one, 0)

    def columns(h):
        return pl.ds(pl.multiple_of(h * HS, HS), HS)

    def send_k(h):
        send_in(h, 0, lambda n: k_stage.at[n], kbuf.at[h, my_col, 1, my_rows])

    def send_v(h):
        send_in(h, 1, lambda n: v_in.at[:, columns(n)], vbuf.at[h, my_col, 1, my_rows])

    def send_q(h):
        send_in(h, 2, lambda n: q_stage.at[n], qbuf.at[h, my_col, my_rows])

    def send_g(h):
        send_in(h, 3, lambda n: g_in.at[:, columns(n)], gbuf.at[h, my_col, my_rows])

    normalize(k_in, k_gain, k_stage, k_fac)
    pl.semaphore_wait(
        barrier, NH - 1 + has_low.astype(jnp.int32) + has_high.astype(jnp.int32)
    )
    send_v(0)
    send_k(0)
    normalize(q_in, q_gain, q_stage, q_fac)
    send_q(0)
    send_g(0)

    def rest(h, carry):
        send_k(h)
        send_v(h)
        send_q(h)
        send_g(h)
        return carry

    lax.fori_loop(1, HPD, rest, 0)

    def halo_copy(h, which, up):
        buf = (kbuf, vbuf)[which]
        side = 1 - up
        side = 0 if up else 1
        return pltpu.make_async_remote_copy(
            src_ref=buf.at[h, :, 1],
            dst_ref=buf.at[h, :, 0 if up else 2],
            send_sem=halo_send.at[h, which, side],
            recv_sem=halo_recv.at[h, which, side],
            device_id={"blk": b + 1 if up else b - 1},
        )

    def forward(h):
        wait_for(kbuf.at[h, :, 1], in_recv.at[0, h])
        wait_for(vbuf.at[h, :, 1], in_recv.at[1, h])
        for which in range(2):

            @pl.when(has_high)
            def _():
                halo_copy(h, which, True).start()

            @pl.when(has_low)
            def _():
                halo_copy(h, which, False).start()

    def await_halo(h):
        for which in range(2):

            @pl.when(has_low)
            def _():
                halo_copy(h, which, True).wait_recv()

            @pl.when(has_high)
            def _():
                halo_copy(h, which, False).wait_recv()

    def send_back(which, src, dst, t):
        @pl.when(t == g)
        def _():
            pltpu.make_async_copy(src, dst, back_recv.at[which]).start()

        @pl.when(t != g)
        def _():
            pltpu.make_async_remote_copy(
                src_ref=src,
                dst_ref=dst,
                send_sem=back_send.at[which],
                recv_sem=back_recv.at[which],
                device_id={"head": t},
            ).start()

    def attend(h, c):
        low = jnp.maximum(c - 1, 0) * 3
        high = jnp.minimum(c + 2, COLS) * 3
        q = qbuf[h, c]

        def first(j, top):
            s = nt(kbuf[h, j // 3, j % 3], q)
            s_buf[j - low] = s
            away = bias[c * 12 + j]
            top = jnp.maximum(top, jnp.max(s[:TILE], axis=0, keepdims=True) + away[0:1])
            return jnp.maximum(top, jnp.max(s[TILE:], axis=0, keepdims=True) + away[1:2])

        top = lax.fori_loop(low, high, first, jnp.full((1, CH), 2 * FAR, f32)) * SCALE2

        def second(j, carry):
            total, out = carry
            away = bias[c * 12 + j]
            s = s_buf[j - low]
            e0 = jnp.exp2(s[:TILE] * SCALE2 - (top - away[0:1]))
            e1 = jnp.exp2(s[TILE:] * SCALE2 - (top - away[1:2]))
            total = total + jnp.sum(e0, axis=0, keepdims=True) + jnp.sum(e1, axis=0, keepdims=True)
            e = jnp.concatenate([e0.astype(bf16), e1.astype(bf16)], axis=0)
            p_buf[j - low] = e
            return total, out + nn(vt_buf[j], e)

        total, out = lax.fori_loop(
            low, high, second, (jnp.zeros((1, CH), f32), jnp.zeros((HS, CH), f32))
        )
        inverse = 1.0 / total
        out = out * inverse
        o_send[h, c] = out.T.astype(bf16)
        grad = gbuf[h, c].astype(f32).T
        delta = jnp.sum(out * grad, axis=0, keepdims=True) * inverse
        grad = grad * inverse
        grad_t = grad.astype(bf16)
        grad_s = grad.T.astype(bf16)

        def third(j, dq):
            e = p_buf[j - low]
            dp = nn(vbuf[h, j // 3, j % 3], grad_t)
            ds = (e.astype(f32) * (dp - delta)).astype(bf16)
            acc_v[j] += nn(e, grad_s)
            acc_k[j] += nn(ds, q)
            return dq + nn(kt_buf[j], ds)

        dq = lax.fori_loop(low, high, third, jnp.zeros((HS, CH), f32))
        dq_send[h, c] = (dq * SCALE).T.astype(bf16)
        for r in range(2):
            rows = pl.ds(r * TILE, TILE)
            t = r * COLS + c
            send_back(0, o_send.at[h, c, rows], att_out.at[:, columns(g * HPD + h)], t)
            send_back(1, dq_send.at[h, c, rows], dq_recv.at[g * HPD + h], t)

    def edge_copy(e, up):
        return pltpu.make_async_remote_copy(
            src_ref=edge_send.at[e, 1 if up else 0],
            dst_ref=edge_recv.at[e, 0 if up else 1],
            send_sem=edge_ssem.at[e, 1 if up else 0],
            recv_sem=edge_rsem.at[e, 0 if up else 1],
            device_id={"blk": b + 1 if up else b - 1},
        )

    def finish(h, c):
        e = h * COLS + c
        for side, slab in ((0, 0), (1, 2)):
            edge_send[e, side, 0] = (acc_k[c * 3 + slab] * SCALE).astype(bf16)
            edge_send[e, side, 1] = acc_v[c * 3 + slab].astype(bf16)
        own_acc[e, 0] = acc_k[c * 3 + 1] * SCALE
        own_acc[e, 1] = acc_v[c * 3 + 1]

        @pl.when(has_high)
        def _():
            edge_copy(e, True).start()

        @pl.when(has_low)
        def _():
            edge_copy(e, False).start()

    def settle(h, c):
        e = h * COLS + c

        @pl.when(has_low)
        def _():
            edge_copy(e, True).wait_recv()

        @pl.when(has_high)
        def _():
            edge_copy(e, False).wait_recv()

        for a in range(2):
            own_send[e, a] = (
                own_acc[e, a] + edge_recv[e, 0, a].astype(f32) + edge_recv[e, 1, a].astype(f32)
            ).astype(bf16)
        for r in range(2):
            rows = pl.ds(r * TILE, TILE)
            t = r * COLS + c
            send_back(2, own_send.at[e, 0, rows], dk_recv.at[g * HPD + h], t)
            send_back(3, own_send.at[e, 1, rows], vgrad_out.at[:, columns(g * HPD + h)], t)

    def start_head(h):
        await_halo(h)
        wait_for(qbuf.at[h], in_recv.at[2, h])
        wait_for(gbuf.at[h], in_recv.at[3, h])

        def turn(j, carry):
            kt_buf[j] = kbuf[h, j // 3, j % 3].T
            vt_buf[j] = vbuf[h, j // 3, j % 3].T
            acc_k[j] = jnp.zeros((CH, HS), f32)
            acc_v[j] = jnp.zeros((CH, HS), f32)
            return carry

        lax.fori_loop(0, 3 * COLS, turn, 0)

    forward(0)

    def step(s, carry):
        h, c = s // COLS, s % COLS

        @pl.when(c == 0)
        def _():
            start_head(h)

        @pl.when((c == 1) & (h < HPD - 1))
        def _():
            forward(h + 1)

        attend(h, c)

        @pl.when(c > 0)
        def _():
            finish(h, c - 1)

        @pl.when(c == COLS - 1)
        def _():
            finish(h, COLS - 1)

        @pl.when(h > 0)
        def _():
            settle(h - 1, c)

        return carry

    lax.fori_loop(0, HPD * COLS, step, 0)

    def last(c, carry):
        settle(HPD - 1, c)
        return carry

    lax.fori_loop(0, COLS, last, 0)

    def norm_back(index, x_in, gain, fac, d_recv, grad_out):
        gain_acc[...] = jnp.zeros((8, F), f32)

        def block(i, carry):
            rows = pl.ds(pl.multiple_of(i * ROWS, ROWS), ROWS)
            factor = fac[rows, :]
            total = jnp.zeros((ROWS, HS), f32)
            for h in range(HEADS):
                lanes = slice(h * HS, (h + 1) * HS)
                hat = x_in[rows, lanes].astype(f32) * factor
                product = d_recv[h, rows, :].astype(f32) * hat
                total = total + product * gain[:, lanes]
                gain_acc[:, lanes] += product[:8] + product[8:]
            inner = jnp.sum(total, axis=1, keepdims=True) * (1.0 / F)
            for h in range(HEADS):
                lanes = slice(h * HS, (h + 1) * HS)
                hat = x_in[rows, lanes].astype(f32) * factor
                scaled = d_recv[h, rows, :].astype(f32) * gain[:, lanes]
                grad_out[rows, lanes] = (factor * (scaled - hat * inner)).astype(bf16)
            return carry

        lax.fori_loop(0, TILE // ROWS, block, 0)
        gain_out[index : index + 1, :] = jnp.sum(gain_acc[...], axis=0, keepdims=True)

    wait_for(dq_recv, back_recv.at[1])
    norm_back(0, q_in, q_gain, q_fac, dq_recv, qgrad_out)
    wait_for(dk_recv, back_recv.at[2])
    norm_back(1, k_in, k_gain, k_fac, dk_recv, kgrad_out)
    wait_for(att_out, back_recv.at[0])
    wait_for(vgrad_out, back_recv.at[3])

    sent = dq_recv.at[0 : HEADS - HPD]
    for which in range(4):
        wait_for(sent, in_send.at[which])
        wait_for(sent, back_send.at[which])

    def drain(h, carry):
        for which in range(2):

            @pl.when(has_high)
            def _():
                halo_copy(h, which, True).wait_send()

            @pl.when(has_low)
            def _():
                halo_copy(h, which, False).wait_send()

        return carry

    lax.fori_loop(0, HPD, drain, 0)

    def drain_edges(e, carry):
        @pl.when(has_high)
        def _():
            edge_copy(e, True).wait_send()

        @pl.when(has_low)
        def _():
            edge_copy(e, False).wait_send()

        return carry

    lax.fori_loop(0, HPD * COLS, drain_edges, 0)


def bias_table(tile_lists, tile_counts):
    per_slab = 2 * COLS
    slab = lax.axis_index("blk")
    lists = lax.dynamic_slice_in_dim(tile_lists, slab * per_slab, per_slab, 0)
    counts = lax.dynamic_slice_in_dim(tile_counts, slab * per_slab, per_slab, 0)
    relative = lists - (slab - 1) * per_slab
    live = jnp.arange(KMAX)[None, :] < counts[:, None]
    named = (relative[:, :, None] == jnp.arange(3 * per_slab)[None, None, :]) & live[:, :, None]
    table = jnp.where(jnp.any(named, axis=1), 0.0, FAR).astype(f32)
    table = table.reshape(2, COLS, 3, 2, COLS).transpose(1, 4, 2, 3, 0)
    return jnp.repeat(table.reshape(COLS * 12, 2, 2), TILE, axis=2)


def shards(
    query_input, key_input, value_input, output_grad, query_gain, key_gain, tile_lists, tile_counts
):
    table = bias_table(tile_lists[0], tile_counts[0])
    vmem = pl.BlockSpec(memory_space=pltpu.VMEM)
    anywhere = pl.BlockSpec(memory_space=pl.ANY)
    token = jax.ShapeDtypeStruct((TILE, F), bf16)
    n = HPD * COLS
    attention, query_grad, key_grad, value_grad, gains = pl.pallas_call(
        kernel,
        name="tiles",
        out_shape=(token, token, token, token, jax.ShapeDtypeStruct((2, F), f32)),
        in_specs=[vmem] * 7,
        out_specs=(anywhere, vmem, vmem, anywhere, vmem),
        scratch_shapes=[
            pltpu.VMEM((HEADS, TILE, HS), bf16),
            pltpu.VMEM((HEADS, TILE, HS), bf16),
            pltpu.VMEM((TILE, HS), f32),
            pltpu.VMEM((TILE, HS), f32),
            pltpu.VMEM((HPD, COLS, CH, HS), bf16),
            pltpu.VMEM((HPD, COLS, CH, HS), bf16),
            pltpu.VMEM((HPD, COLS, 3, CH, HS), bf16),
            pltpu.VMEM((HPD, COLS, 3, CH, HS), bf16),
            pltpu.VMEM((12, HS, CH), bf16),
            pltpu.VMEM((12, HS, CH), bf16),
            pltpu.VMEM((9, CH, CH), f32),
            pltpu.VMEM((9, CH, CH), bf16),
            pltpu.VMEM((12, CH, HS), f32),
            pltpu.VMEM((12, CH, HS), f32),
            pltpu.VMEM((n, 2, CH, HS), f32),
            pltpu.VMEM((n, 2, 2, CH, HS), bf16),
            pltpu.VMEM((n, 2, 2, CH, HS), bf16),
            pltpu.VMEM((n, 2, CH, HS), bf16),
            pltpu.VMEM((HPD, COLS, CH, HS), bf16),
            pltpu.VMEM((HPD, COLS, CH, HS), bf16),
            pltpu.VMEM((HEADS, TILE, HS), bf16),
            pltpu.VMEM((HEADS, TILE, HS), bf16),
            pltpu.VMEM((8, F), f32),
            pltpu.SemaphoreType.DMA((4,)),
            pltpu.SemaphoreType.DMA((4, HPD)),
            pltpu.SemaphoreType.DMA((HPD, 2, 2)),
            pltpu.SemaphoreType.DMA((HPD, 2, 2)),
            pltpu.SemaphoreType.DMA((n, 2)),
            pltpu.SemaphoreType.DMA((n, 2)),
            pltpu.SemaphoreType.DMA((4,)),
            pltpu.SemaphoreType.DMA((4,)),
        ],
        compiler_params=pltpu.CompilerParams(
            collective_id=0, has_side_effects=True, vmem_limit_bytes=62 * 1024 * 1024
        ),
    )(
        query_input[0],
        key_input[0],
        value_input[0],
        output_grad[0],
        query_gain[None],
        key_gain[None],
        table,
    )
    gain_grads = lax.psum_scatter(gains, ("dp", "blk", "head"), scatter_dimension=1, tiled=True)
    return (
        attention[None],
        query_grad[None],
        key_grad[None],
        value_grad[None],
        gain_grads[0],
        gain_grads[1],
    )


def solution(mesh):
    tokens = P("dp", ("blk", "head"), None)
    features = P(("dp", "blk", "head"))
    return jax.shard_map(
        shards,
        mesh=mesh,
        in_specs=(tokens, tokens, tokens, tokens, P(), P(), P("dp", None, None), P("dp", None)),
        out_specs=(tokens, tokens, tokens, tokens, features, features),
        check_vma=False,
    )
```

time: 822 us -> 320 us (0.39); the launches traced: 812 us -> 320 us
  Pallas kernels: 0 us -> 233 us
  other arithmetic: 202 us -> 0.12 us
  waiting for transfers between devices: 187 us -> 0 us
  local copies, waits for them, and re-layouts: 167 us -> 10.5 us
  matrix products: 130 us -> 0 us
  starting transfers between devices: 51.6 us -> 0 us
  blocking collectives: 65.8 us -> 76 us
    pallas_call x0 -> x1, Pallas kernels: none -> 233 us  [shards(): pl.pallas_call(kernel, name='tiles', out_shape=(token, token, token, toke...]
    all_to_all x8 -> x0, waiting for transfers between devices: 187 us -> none  [the longest x1 90.2 us: shards(): lax.all_to_all(query_att_heads, 'head', split_axis=0, concat_axis=1, tile...]
    scatter-add x16 -> x0, other arithmetic: 143 us -> none  [the longest x8 75.7 us: visit(): totals.at[1, :, targets]]
    dot_general x40 -> x0, matrix products: 91 us -> none  [the longest x8 30.1 us: tile_step(): jnp.einsum('hqd,hkd->hqk', grad_tile, value_block, preferred_element_type...]
    reshape x23 -> x2, local copies, waits for them, and re-layouts: 44 us -> 1.18 us  [bias_table(): return jnp.repeat(table.reshape(COLS * 12, 2, 2), TILE, axis=2)]
    sub x8 -> x0, matrix products: 39.5 us -> none  [tile_step(): exponent = jnp.exp(scores - row_max)]
    all_to_all x8 -> x0, starting transfers between devices: 37.5 us -> none  [the longest x1 6.88 us: shards(): lax.all_to_all(value_input[0], 'head', split_axis=1, concat_axis=0, tiled...]
    gather x8 -> x0, local copies, waits for them, and re-layouts: 33.9 us -> none  [visit(): jnp.take(padded_grid, targets, axis=2).reshape(2, heads_here, span, HS)]
  transfers between devices with their start and end apart: 12 -> 0, of which waited for: 5 -> 0; matrix products, arithmetic and copies ran while one was open for 9% -> 0% of each run, Pallas kernels for 0% -> 0%
where the time goes in v1:
time: 320 us
  Pallas kernels  233 us (73%)
  blocking collectives  76 us (24%)
  local copies, waits for them, and re-layouts  10.5 us (3%)
    pallas_call x1, Pallas kernels, shards(): pl.pallas_call(kernel, name='tiles', out_shape=(token, token, token, toke...  233 us
    unnamed x1, blocking collectives  76 us
    unnamed x14, local copies, waits for them, and re-layouts  7.7 us

profile of v1, /device:TPU:1, one launch (start us, length us, event | category | flops | bytes accessed | tf_op | source)
XLA Modules:
  0.0 320.1 jit_solution(882828757505471407)
XLA Ops:
  0.6 0.0 copy-start
  0.7 0.7 copy-done
  1.3 0.1 constant_dynamic-slice_fusion.1
  1.4 0.1 copy.30
  1.5 0.1 copy.23
  1.6 0.7 dynamic-slice_bitcast_fusion
  2.3 0.1 fusion.1
  2.4 0.1 select_n.14
  2.5 0.3 copy.28
  2.8 0.2 broadcast_in_dim.38
  3.0 0.9 reshape.58.bias
  3.9 232.7 %tiles.1 = (bf16[192,3072]{1,0:T(8,128)(2,1)}, bf16[192,3072]{1,0:T(8,128)(2,1)}, bf16[192,3072]{1,0:T(8,128)(2,1)}, bf16[192,3072]{1,0:T(8,128)(2,1)}, f32[2,3072]{1,0:T(2,128)}) custom-call(bf16[192,3072]{1,0:T(8,128)(2,1)} %bitcast.26, bf16[192,3072]{1,0:T(8,128)(2,1)} %bitcast.27, bf16[192,3072]{1,0:T(8,128)(2,1)} %bitcast.28, ...), custom_call_target="tpu_custom_call" | custom-call | tf_op jit(solution)/shard_map/tiles/pallas_call | solution.py:486
  236.6 76.0 %all-reduce = f32[2,3072]{1,0:T(2,128)S(1)} all-reduce(f32[2,3072]{1,0:T(2,128)} %get-tuple-element.15), channel_id=2, replica_groups=mesh['dp'=2,'blk'=8,'head'=8] {'dp','blk','head'}, use_global_device_ids=true, to_apply=%region_1.2.clone | all-reduce | flops 6144 | bytes 49152
  312.6 0.1 constant_dynamic-slice_fusion
  312.7 0.5 slice_bitcast_fusion
  313.2 0.0 copy-start.3
  313.2 2.5 copy.35
  315.7 0.0 copy-done.3
  315.7 0.0 copy-start.2
  315.7 1.0 copy.36
  316.7 0.7 copy-done.2
  317.4 1.0 copy.37
  318.4 0.7 copy-done.1
  319.1 1.0 copy.38
  (4 shorter events, 0.0 us)
Async XLA Ops:
  0.6 0.7 copy-start
  313.2 2.5 copy-start.3
  315.7 1.7 copy-start.2
  317.4 1.7 copy-start.1

commit v2 on v1

--- a/solution.py
+++ b/solution.py
@@ -32,6 +32,11 @@
 
 def nt(a, b):
     return lax.dot_general(a, b, (((1,), (1,)), ((), ())), preferred_element_type=f32)
+
+
+def group_of(slab, device):
+    low = device % 2
+    return device - low + (low + slab // 4) % 2
 
 
 def wait_for(ref, sem):
@@ -73,7 +78,9 @@
     dq_send,
     dq_recv,
     dk_recv,
-    gain_acc,
+    gain_tab,
+    gain_recv,
+    gain_sem,
     in_send,
     in_recv,
     halo_send,
@@ -83,29 +90,58 @@
     back_send,
     back_recv,
 ):
+    d = lax.axis_index("dp")
     b = lax.axis_index("blk")
-    g = lax.axis_index("head")
+    tile = lax.axis_index("head")
+    g = group_of(b, tile)
     has_low = b > 0
     has_high = b < NB - 1
-    my_row = g // COLS
-    my_col = g % COLS
+    below = {"blk": b - 1, "head": group_of(b - 1, g)}
+    above = {"blk": b + 1, "head": group_of(b + 1, g)}
+    my_row = tile // COLS
+    my_col = tile % COLS
+    gain_group = d * 4 + b // 2
+    gain_self = gain_group == g
     my_rows = pl.ds(pl.multiple_of(my_row * TILE, TILE), TILE)
 
     barrier = pltpu.get_barrier_semaphore()
 
     def greet(i, carry):
-        pl.semaphore_signal(barrier, inc=1, device_id={"head": (g + i) % NH})
+        pl.semaphore_signal(barrier, inc=1, device_id={"head": (tile + i) % NH})
         return carry
 
     lax.fori_loop(1, NH, greet, 0)
+
+    def gain_target(j):
+        return {"dp": g // 4, "blk": 2 * (g % 4) + j // NH, "head": j % NH}
+
+    def gain_target_is_me(j):
+        return (g // 4 == d) & (2 * (g % 4) + j // NH == b) & (j % NH == tile)
+
+    def greet_gain(j, carry):
+        @pl.when(jnp.logical_not(gain_target_is_me(j)))
+        def _():
+            pl.semaphore_signal(barrier, inc=1, device_id=gain_target(j))
+
+        @pl.when(jnp.logical_not((j // NB == d) & (j % NB == b) & gain_self))
+        def _():
+            pl.semaphore_signal(
+                barrier,
+                inc=1,
+                device_id={"dp": j // NB, "blk": j % NB, "head": group_of(j % NB, gain_group)},
+            )
+
+        return carry
+
+    lax.fori_loop(0, 2 * NB, greet_gain, 0)
 
     @pl.when(has_low)
     def _():
-        pl.semaphore_signal(barrier, inc=1, device_id={"blk": b - 1})
+        pl.semaphore_signal(barrier, inc=1, device_id=below)
 
     @pl.when(has_high)
     def _():
-        pl.semaphore_signal(barrier, inc=1, device_id={"blk": b + 1})
+        pl.semaphore_signal(barrier, inc=1, device_id=above)
 
     def clear_side(slab, side):
         zeros = jnp.zeros((CH, HS), bf16)
@@ -150,9 +186,9 @@
         here.start()
 
         def one(i, carry):
-            to = (g + i) % NH
+            to = (tile + i) % NH
             pltpu.make_async_remote_copy(
-                src_ref=src_of(to * HPD + h),
+                src_ref=src_of(group_of(b, to) * HPD + h),
                 dst_ref=dst,
                 send_sem=in_send.at[which],
                 recv_sem=in_recv.at[which, h],
@@ -179,7 +215,13 @@
 
     normalize(k_in, k_gain, k_stage, k_fac)
     pl.semaphore_wait(
-        barrier, NH - 1 + has_low.astype(jnp.int32) + has_high.astype(jnp.int32)
+        barrier,
+        NH
+        - 1
+        + 4 * NB
+        - 2 * gain_self.astype(jnp.int32)
+        + has_low.astype(jnp.int32)
+        + has_high.astype(jnp.int32),
     )
     send_v(0)
     send_k(0)
@@ -198,14 +240,13 @@
 
     def halo_copy(h, which, up):
         buf = (kbuf, vbuf)[which]
-        side = 1 - up
         side = 0 if up else 1
         return pltpu.make_async_remote_copy(
             src_ref=buf.at[h, :, 1],
             dst_ref=buf.at[h, :, 0 if up else 2],
             send_sem=halo_send.at[h, which, side],
             recv_sem=halo_recv.at[h, which, side],
-            device_id={"blk": b + 1 if up else b - 1},
+            device_id=above if up else below,
         )
 
     def forward(h):
@@ -233,11 +274,11 @@
                 halo_copy(h, which, False).wait_recv()
 
     def send_back(which, src, dst, t):
-        @pl.when(t == g)
+        @pl.when(t == tile)
         def _():
             pltpu.make_async_copy(src, dst, back_recv.at[which]).start()
 
-        @pl.when(t != g)
+        @pl.when(t != tile)
         def _():
             pltpu.make_async_remote_copy(
                 src_ref=src,
@@ -293,7 +334,9 @@
             return dq + nn(kt_buf[j], ds)
 
         dq = lax.fori_loop(low, high, third, jnp.zeros((HS, CH), f32))
-        dq_send[h, c] = (dq * SCALE).T.astype(bf16)
+        dq = (dq * SCALE).T.astype(bf16)
+        dq_send[h, c] = dq
+        gain_tab[h, 0:1, :] += jnp.sum(dq.astype(f32) * q.astype(f32), axis=0, keepdims=True)
         for r in range(2):
             rows = pl.ds(r * TILE, TILE)
             t = r * COLS + c
@@ -306,7 +349,7 @@
             dst_ref=edge_recv.at[e, 0 if up else 1],
             send_sem=edge_ssem.at[e, 1 if up else 0],
             recv_sem=edge_rsem.at[e, 0 if up else 1],
-            device_id={"blk": b + 1 if up else b - 1},
+            device_id=above if up else below,
         )
 
     def finish(h, c):
@@ -340,6 +383,8 @@
             own_send[e, a] = (
                 own_acc[e, a] + edge_recv[e, 0, a].astype(f32) + edge_recv[e, 1, a].astype(f32)
             ).astype(bf16)
+        product = own_send[e, 0].astype(f32) * kbuf[h, c, 1].astype(f32)
+        gain_tab[h, 1:2, :] += jnp.sum(product, axis=0, keepdims=True)
         for r in range(2):
             rows = pl.ds(r * TILE, TILE)
             t = r * COLS + c
@@ -360,6 +405,7 @@
 
         lax.fori_loop(0, 3 * COLS, turn, 0)
 
+    gain_tab[...] = jnp.zeros_like(gain_tab)
     forward(0)
 
     def step(s, carry):
@@ -397,9 +443,33 @@
 
     lax.fori_loop(0, COLS, last, 0)
 
-    def norm_back(index, x_in, gain, fac, d_recv, grad_out):
-        gain_acc[...] = jnp.zeros((8, F), f32)
-
+    for h in range(HPD):
+        for row, gain in ((0, q_gain), (1, k_gain)):
+            gain_tab[h, row : row + 1, :] = gain_tab[h, row : row + 1, :] / gain[:, columns(g * HPD + h)]
+
+    def give(j, carry):
+        dst = gain_recv.at[d * NB + b]
+        me = gain_target_is_me(j)
+
+        @pl.when(me)
+        def _():
+            pltpu.make_async_copy(gain_tab, dst, gain_sem.at[1]).start()
+
+        @pl.when(jnp.logical_not(me))
+        def _():
+            pltpu.make_async_remote_copy(
+                src_ref=gain_tab,
+                dst_ref=dst,
+                send_sem=gain_sem.at[0],
+                recv_sem=gain_sem.at[1],
+                device_id=gain_target(j),
+            ).start()
+
+        return carry
+
+    lax.fori_loop(0, 2 * NB, give, 0)
+
+    def norm_back(x_in, gain, fac, d_recv, grad_out):
         def block(i, carry):
             rows = pl.ds(pl.multiple_of(i * ROWS, ROWS), ROWS)
             factor = fac[rows, :]
@@ -409,7 +479,6 @@
                 hat = x_in[rows, lanes].astype(f32) * factor
                 product = d_recv[h, rows, :].astype(f32) * hat
                 total = total + product * gain[:, lanes]
-                gain_acc[:, lanes] += product[:8] + product[8:]
             inner = jnp.sum(total, axis=1, keepdims=True) * (1.0 / F)
             for h in range(HEADS):
                 lanes = slice(h * HS, (h + 1) * HS)
@@ -419,14 +488,33 @@
             return carry
 
         lax.fori_loop(0, TILE // ROWS, block, 0)
-        gain_out[index : index + 1, :] = jnp.sum(gain_acc[...], axis=0, keepdims=True)
 
     wait_for(dq_recv, back_recv.at[1])
-    norm_back(0, q_in, q_gain, q_fac, dq_recv, qgrad_out)
+    norm_back(q_in, q_gain, q_fac, dq_recv, qgrad_out)
     wait_for(dk_recv, back_recv.at[2])
-    norm_back(1, k_in, k_gain, k_fac, dk_recv, kgrad_out)
+    norm_back(k_in, k_gain, k_fac, dk_recv, kgrad_out)
+    wait_for(gain_recv, gain_sem.at[1])
+    start = 24 * ((b % 2) * NH + tile)
+    lane = lax.broadcasted_iota(jnp.int32, (HS, HS), 1)
+    source = lax.broadcasted_iota(jnp.int32, (HS, HS), 0)
+    sums = jnp.zeros((8, HS), f32)
+    for h in range(HPD):
+        pick = ((source + h * HS == lane + start) & (lane < 24)).astype(f32)
+        part = gain_recv[0, h]
+        for i in range(1, 2 * NB):
+            part = part + gain_recv[i, h]
+        sums = sums + jnp.dot(
+            part, pick, precision=lax.Precision.HIGHEST, preferred_element_type=f32
+        )
+    gain_out[...] = sums
     wait_for(att_out, back_recv.at[0])
     wait_for(vgrad_out, back_recv.at[3])
+
+    wait_for(gain_recv.at[0 : 2 * NB - 1], gain_sem.at[0])
+
+    @pl.when(jnp.logical_not(gain_self))
+    def _():
+        wait_for(gain_recv.at[0], gain_sem.at[0])
 
     sent = dq_recv.at[0 : HEADS - HPD]
     for which in range(4):
@@ -486,7 +574,7 @@
     attention, query_grad, key_grad, value_grad, gains = pl.pallas_call(
         kernel,
         name="tiles",
-        out_shape=(token, token, token, token, jax.ShapeDtypeStruct((2, F), f32)),
+        out_shape=(token, token, token, token, jax.ShapeDtypeStruct((8, HS), f32)),
         in_specs=[vmem] * 7,
         out_specs=(anywhere, vmem, vmem, anywhere, vmem),
         scratch_shapes=[
@@ -512,7 +600,9 @@
             pltpu.VMEM((HPD, COLS, CH, HS), bf16),
             pltpu.VMEM((HEADS, TILE, HS), bf16),
             pltpu.VMEM((HEADS, TILE, HS), bf16),
-            pltpu.VMEM((8, F), f32),
+            pltpu.VMEM((HPD, 8, HS), f32),
+            pltpu.VMEM((2 * NB, HPD, 8, HS), f32),
+            pltpu.SemaphoreType.DMA((2,)),
             pltpu.SemaphoreType.DMA((4,)),
             pltpu.SemaphoreType.DMA((4, HPD)),
             pltpu.SemaphoreType.DMA((HPD, 2, 2)),
@@ -534,14 +624,14 @@
         key_gain[None],
         table,
     )
-    gain_grads = lax.psum_scatter(gains, ("dp", "blk", "head"), scatter_dimension=1, tiled=True)
+    width = F // (2 * NB * NH)
     return (
         attention[None],
         query_grad[None],
         key_grad[None],
         value_grad[None],
-        gain_grads[0],
-        gain_grads[1],
+        gains[0, :width],
+        gains[1, :width],
     )
 
 

time: 320 us -> 188 us (0.59)
  the two profiles are of different devices: /device:TPU:1 before, /device:TPU:57 now
where the time goes in v2:
time: 188 us; the launch traced here: 187 us
  Pallas kernels  175 us (93%)
  local copies, waits for them, and re-layouts  11.2 us (6%)
    pallas_call x1, Pallas kernels, shards(): pl.pallas_call(kernel, name='tiles', out_shape=(token, token, token, toke...  175 us
    unnamed x13, local copies, waits for them, and re-layouts  7.63 us

profile of v2, /device:TPU:57, one launch (start us, length us, event | category | flops | bytes accessed | tf_op | source)
XLA Modules:
  0.0 187.4 jit_solution(14368528109030704799)
XLA Ops:
  0.6 0.0 copy-start
  0.7 0.7 copy-done
  1.3 0.1 constant_dynamic-slice_fusion
  1.4 0.1 copy.25
  1.5 0.1 copy.20
  1.6 0.7 dynamic-slice_bitcast_fusion
  2.3 0.1 fusion.1
  2.4 0.1 select_n.14
  2.5 0.3 copy.23
  2.8 0.2 broadcast_in_dim.38
  3.0 0.9 reshape.58.bias
  3.9 175.4 %tiles.1 = (bf16[192,3072]{1,0:T(8,128)(2,1)}, bf16[192,3072]{1,0:T(8,128)(2,1)}, bf16[192,3072]{1,0:T(8,128)(2,1)}, bf16[192,3072]{1,0:T(8,128)(2,1)}, f32[8,128]{1,0:T(8,128)}) custom-call(bf16[192,3072]{1,0:T(8,128)(2,1)} %bitcast.24, bf16[192,3072]{1,0:T(8,128)(2,1)} %bitcast.25, bf16[192,3072]{1,0:T(8,128)(2,1)} %bitcast.26, ...), custom_call_target="tpu_custom_call" | custom-call | tf_op jit(solution)/shard_map/tiles/pallas_call | solution.py:574
  179.3 1.3 slice_bitcast_fusion
  180.6 0.0 copy-start.3
  180.6 2.5 %copy.30 = bf16[1,192,3072]{2,1,0:T(8,128)(2,1)} copy(bf16[1,192,3072]{2,1,0:T(8,128)(2,1)} %bitcast.23) | data formatting | bytes 2359296
  183.0 0.0 copy-done.3
  183.0 0.0 copy-start.2
  183.0 1.0 copy.31
  184.0 0.7 copy-done.2
  184.7 0.0 copy-start.1
  184.7 1.0 copy.32
  185.7 0.7 copy-done.1
  186.4 1.0 copy.33
  (3 shorter events, 0.0 us)
Async XLA Ops:
  0.6 0.7 copy-start
  180.6 2.5 %copy-start.3 = (bf16[192,3072]{1,0:T(8,128)(2,1)S(1)}, bf16[192,3072]{1,0:T(8,128)(2,1)}, u32[]{:S(2)}) copy-start(bf16[192,3072]{1,0:T(8,128)(2,1)} %get-tuple-element.12) | copy-start | bytes 3538948
  183.0 1.7 copy-start.2
  184.7 1.7 copy-start.1

commit v3 on v2

--- a/solution.py
+++ b/solution.py
@@ -68,6 +68,7 @@
     vt_buf,
     s_buf,
     p_buf,
+    ds_buf,
     acc_k,
     acc_v,
     own_acc,
@@ -229,15 +230,6 @@
     send_q(0)
     send_g(0)
 
-    def rest(h, carry):
-        send_k(h)
-        send_v(h)
-        send_q(h)
-        send_g(h)
-        return carry
-
-    lax.fori_loop(1, HPD, rest, 0)
-
     def halo_copy(h, which, up):
         buf = (kbuf, vbuf)[which]
         side = 0 if up else 1
@@ -289,29 +281,33 @@
             ).start()
 
     def attend(h, c):
-        low = jnp.maximum(c - 1, 0) * 3
-        high = jnp.minimum(c + 2, COLS) * 3
+        low = jnp.maximum(c - 1, 0)
+        high = jnp.minimum(c + 2, COLS)
         q = qbuf[h, c]
 
-        def first(j, top):
-            s = nt(kbuf[h, j // 3, j % 3], q)
-            s_buf[j - low] = s
-            away = bias[c * 12 + j]
-            top = jnp.maximum(top, jnp.max(s[:TILE], axis=0, keepdims=True) + away[0:1])
-            return jnp.maximum(top, jnp.max(s[TILE:], axis=0, keepdims=True) + away[1:2])
+        def first(k, top):
+            for slab in range(3):
+                s = nt(kbuf[h, k, slab], q)
+                s_buf[k - low, slab] = s
+                away = bias[c * 12 + k * 3 + slab]
+                top = jnp.maximum(top, jnp.max(s[:TILE], axis=0, keepdims=True) + away[0:1])
+                top = jnp.maximum(top, jnp.max(s[TILE:], axis=0, keepdims=True) + away[1:2])
+            return top
 
         top = lax.fori_loop(low, high, first, jnp.full((1, CH), 2 * FAR, f32)) * SCALE2
 
-        def second(j, carry):
+        def second(k, carry):
             total, out = carry
-            away = bias[c * 12 + j]
-            s = s_buf[j - low]
-            e0 = jnp.exp2(s[:TILE] * SCALE2 - (top - away[0:1]))
-            e1 = jnp.exp2(s[TILE:] * SCALE2 - (top - away[1:2]))
-            total = total + jnp.sum(e0, axis=0, keepdims=True) + jnp.sum(e1, axis=0, keepdims=True)
-            e = jnp.concatenate([e0.astype(bf16), e1.astype(bf16)], axis=0)
-            p_buf[j - low] = e
-            return total, out + nn(vt_buf[j], e)
+            for slab in range(3):
+                away = bias[c * 12 + k * 3 + slab]
+                s = s_buf[k - low, slab]
+                e0 = jnp.exp2(s[:TILE] * SCALE2 - (top - away[0:1]))
+                e1 = jnp.exp2(s[TILE:] * SCALE2 - (top - away[1:2]))
+                total = total + jnp.sum(e0, axis=0, keepdims=True)
+                total = total + jnp.sum(e1, axis=0, keepdims=True)
+                p_buf[k - low, slab * CH : slab * CH + TILE] = e0.astype(bf16)
+                p_buf[k - low, slab * CH + TILE : (slab + 1) * CH] = e1.astype(bf16)
+            return total, out + nn(vt_buf[k], p_buf[k - low])
 
         total, out = lax.fori_loop(
             low, high, second, (jnp.zeros((1, CH), f32), jnp.zeros((HS, CH), f32))
@@ -325,13 +321,15 @@
         grad_t = grad.astype(bf16)
         grad_s = grad.T.astype(bf16)
 
-        def third(j, dq):
-            e = p_buf[j - low]
-            dp = nn(vbuf[h, j // 3, j % 3], grad_t)
-            ds = (e.astype(f32) * (dp - delta)).astype(bf16)
-            acc_v[j] += nn(e, grad_s)
-            acc_k[j] += nn(ds, q)
-            return dq + nn(kt_buf[j], ds)
+        def third(k, dq):
+            for slab in range(3):
+                e = p_buf[k - low, slab * CH : (slab + 1) * CH]
+                dp = nn(vbuf[h, k, slab], grad_t)
+                ds = (e.astype(f32) * (dp - delta)).astype(bf16)
+                ds_buf[slab * CH : (slab + 1) * CH] = ds
+                acc_v[k * 3 + slab] += nn(e, grad_s)
+                acc_k[k * 3 + slab] += nn(ds, q)
+            return dq + nn(kt_buf[k], ds_buf[...])
 
         dq = lax.fori_loop(low, high, third, jnp.zeros((HS, CH), f32))
         dq = (dq * SCALE).T.astype(bf16)
@@ -368,8 +366,8 @@
         def _():
             edge_copy(e, False).start()
 
-    def settle(h, c):
-        e = h * COLS + c
+    def settle(e):
+        h, c = e // COLS, e % COLS
 
         @pl.when(has_low)
         def _():
@@ -396,18 +394,29 @@
         wait_for(qbuf.at[h], in_recv.at[2, h])
         wait_for(gbuf.at[h], in_recv.at[3, h])
 
-        def turn(j, carry):
-            kt_buf[j] = kbuf[h, j // 3, j % 3].T
-            vt_buf[j] = vbuf[h, j // 3, j % 3].T
-            acc_k[j] = jnp.zeros((CH, HS), f32)
-            acc_v[j] = jnp.zeros((CH, HS), f32)
+        def turn(k, carry):
+            for slab in range(3):
+                keys = slice(slab * CH, (slab + 1) * CH)
+                kt_buf[k, :, keys] = kbuf[h, k, slab].T
+                vt_buf[k, :, keys] = vbuf[h, k, slab].T
+                acc_k[k * 3 + slab] = jnp.zeros((CH, HS), f32)
+                acc_v[k * 3 + slab] = jnp.zeros((CH, HS), f32)
             return carry
 
-        lax.fori_loop(0, 3 * COLS, turn, 0)
+        lax.fori_loop(0, COLS, turn, 0)
 
     gain_tab[...] = jnp.zeros_like(gain_tab)
     forward(0)
 
+    def rest(h, carry):
+        send_k(h)
+        send_v(h)
+        send_q(h)
+        send_g(h)
+        return carry
+
+    lax.fori_loop(1, HPD, rest, 0)
+
     def step(s, carry):
         h, c = s // COLS, s % COLS
 
@@ -429,19 +438,19 @@
         def _():
             finish(h, COLS - 1)
 
-        @pl.when(h > 0)
-        def _():
-            settle(h - 1, c)
+        @pl.when(s > 1)
+        def _():
+            settle(s - 2)
 
         return carry
 
     lax.fori_loop(0, HPD * COLS, step, 0)
 
-    def last(c, carry):
-        settle(HPD - 1, c)
-        return carry
-
-    lax.fori_loop(0, COLS, last, 0)
+    def last(e, carry):
+        settle(e)
+        return carry
+
+    lax.fori_loop(HPD * COLS - 2, HPD * COLS, last, 0)
 
     for h in range(HPD):
         for row, gain in ((0, q_gain), (1, k_gain)):
@@ -586,10 +595,11 @@
             pltpu.VMEM((HPD, COLS, CH, HS), bf16),
             pltpu.VMEM((HPD, COLS, 3, CH, HS), bf16),
             pltpu.VMEM((HPD, COLS, 3, CH, HS), bf16),
-            pltpu.VMEM((12, HS, CH), bf16),
-            pltpu.VMEM((12, HS, CH), bf16),
-            pltpu.VMEM((9, CH, CH), f32),
-            pltpu.VMEM((9, CH, CH), bf16),
+            pltpu.VMEM((COLS, HS, 3 * CH), bf16),
+            pltpu.VMEM((COLS, HS, 3 * CH), bf16),
+            pltpu.VMEM((3, 3, CH, CH), f32),
+            pltpu.VMEM((3, 3 * CH, CH), bf16),
+            pltpu.VMEM((3 * CH, CH), bf16),
             pltpu.VMEM((12, CH, HS), f32),
             pltpu.VMEM((12, CH, HS), f32),
             pltpu.VMEM((n, 2, CH, HS), f32),

time: 188 us -> 175 us (0.931)
  the two profiles are of different devices: /device:TPU:57 before, /device:TPU:1 now
where the time goes in v3:
time: 175 us; the launch traced here: 174 us
  Pallas kernels  162 us (93%)
  local copies, waits for them, and re-layouts  11.2 us (6%)
    pallas_call x1, Pallas kernels, shards(): pl.pallas_call(kernel, name='tiles', out_shape=(token, token, token, toke...  162 us
    unnamed x13, local copies, waits for them, and re-layouts  7.63 us

profile of v3, /device:TPU:1, one launch (start us, length us, event | category | flops | bytes accessed | tf_op | source)
XLA Modules:
  0.0 174.4 jit_solution(5079142604767927204)
XLA Ops:
  0.6 0.0 copy-start
  0.7 0.7 copy-done
  1.3 0.1 constant_dynamic-slice_fusion
  1.4 0.1 copy.25
  1.5 0.1 copy.20
  1.6 0.7 dynamic-slice_bitcast_fusion
  2.3 0.1 fusion.1
  2.4 0.1 select_n.14
  2.5 0.3 copy.23
  2.8 0.2 broadcast_in_dim.38
  3.0 0.9 reshape.58.bias
  3.9 162.4 %tiles.1 = (bf16[192,3072]{1,0:T(8,128)(2,1)}, bf16[192,3072]{1,0:T(8,128)(2,1)}, bf16[192,3072]{1,0:T(8,128)(2,1)}, bf16[192,3072]{1,0:T(8,128)(2,1)}, f32[8,128]{1,0:T(8,128)}) custom-call(bf16[192,3072]{1,0:T(8,128)(2,1)} %bitcast.24, bf16[192,3072]{1,0:T(8,128)(2,1)} %bitcast.25, bf16[192,3072]{1,0:T(8,128)(2,1)} %bitcast.26, ...), custom_call_target="tpu_custom_call" | custom-call | tf_op jit(solution)/shard_map/tiles/pallas_call | solution.py:583
  166.2 1.3 slice_bitcast_fusion
  167.5 0.0 copy-start.3
  167.5 2.5 %copy.30 = bf16[1,192,3072]{2,1,0:T(8,128)(2,1)} copy(bf16[1,192,3072]{2,1,0:T(8,128)(2,1)} %bitcast.23) | data formatting | bytes 2359296
  170.0 0.0 copy-done.3
  170.0 0.0 copy-start.2
  170.0 1.0 copy.31
  171.0 0.7 copy-done.2
  171.7 0.0 copy-start.1
  171.7 1.0 copy.32
  172.7 0.7 copy-done.1
  173.4 1.0 copy.33
  (3 shorter events, 0.0 us)
Async XLA Ops:
  0.6 0.7 copy-start
  167.5 2.5 %copy-start.3 = (bf16[192,3072]{1,0:T(8,128)(2,1)S(1)}, bf16[192,3072]{1,0:T(8,128)(2,1)}, u32[]{:S(2)}) copy-start(bf16[192,3072]{1,0:T(8,128)(2,1)} %get-tuple-element.12) | copy-start | bytes 3538948
  170.0 1.7 copy-start.2
  171.7 1.7 copy-start.1

commit v4 on v3

--- a/solution.py
+++ b/solution.py
@@ -18,10 +18,12 @@
 F = HEADS * HS
 CH = 2 * TILE
 ROWS = 16
+LAG = 3
 EPSILON = 1e-06
 SCALE = HS**-0.5
 SCALE2 = SCALE * 1.4426950408889634
 FAR = -1e30
+NOWHERE = -1000
 f32 = jnp.float32
 bf16 = jnp.bfloat16
 
@@ -37,6 +39,19 @@
 def group_of(slab, device):
     low = device % 2
     return device - low + (low + slab // 4) % 2
+
+
+def owner(seq, slab):
+    pair, part = slab % 4 // 2, slab % 2
+    x = pair * (2 + seq) + (1 - pair) * (1 - seq)
+    return {"dp": (part + pair) % 2, "blk": slab // 4 * 4 + x}
+
+
+def unit(core, blk):
+    x = blk % 4
+    pair = x // 2
+    seq = pair * (x - 2) + (1 - pair) * (1 - x)
+    return seq, blk // 4 * 4 + 2 * pair + (core + pair) % 2
 
 
 def wait_for(ref, sem):
@@ -50,7 +65,8 @@
     g_in,
     q_gain,
     k_gain,
-    bias,
+    lists,
+    counts,
     att_out,
     qgrad_out,
     kgrad_out,
@@ -79,6 +95,10 @@
     dq_send,
     dq_recv,
     dk_recv,
+    named,
+    named_here,
+    bias,
+    list_sem,
     gain_tab,
     gain_recv,
     gain_sem,
@@ -94,11 +114,15 @@
     d = lax.axis_index("dp")
     b = lax.axis_index("blk")
     tile = lax.axis_index("head")
+    seq, slab_here = unit(d, b)
     g = group_of(b, tile)
-    has_low = b > 0
-    has_high = b < NB - 1
-    below = {"blk": b - 1, "head": group_of(b - 1, g)}
-    above = {"blk": b + 1, "head": group_of(b + 1, g)}
+    has_low = slab_here > 0
+    has_high = slab_here < NB - 1
+    below = {**owner(seq, slab_here - 1), "head": group_of(slab_here - 1, g)}
+    above = {**owner(seq, slab_here + 1), "head": group_of(slab_here + 1, g)}
+    work = owner(d, b)
+    lists_local = seq == d
+    other_core = {"dp": 1 - d}
     my_row = tile // COLS
     my_col = tile % COLS
     gain_group = d * 4 + b // 2
@@ -108,10 +132,12 @@
     barrier = pltpu.get_barrier_semaphore()
 
     def greet(i, carry):
-        pl.semaphore_signal(barrier, inc=1, device_id={"head": (tile + i) % NH})
+        pl.semaphore_signal(barrier, inc=1, device_id={**work, "head": i})
+        pl.semaphore_signal(barrier, inc=1, device_id={"dp": seq, "blk": slab_here, "head": i})
         return carry
 
-    lax.fori_loop(1, NH, greet, 0)
+    lax.fori_loop(0, NH, greet, 0)
+    pl.semaphore_signal(barrier, inc=1, device_id=other_core)
 
     def gain_target(j):
         return {"dp": g // 4, "blk": 2 * (g % 4) + j // NH, "head": j % NH}
@@ -124,12 +150,12 @@
         def _():
             pl.semaphore_signal(barrier, inc=1, device_id=gain_target(j))
 
-        @pl.when(jnp.logical_not((j // NB == d) & (j % NB == b) & gain_self))
+        @pl.when(jnp.logical_not((j // NB == seq) & (j % NB == slab_here) & gain_self))
         def _():
             pl.semaphore_signal(
                 barrier,
                 inc=1,
-                device_id={"dp": j // NB, "blk": j % NB, "head": group_of(j % NB, gain_group)},
+                device_id={**owner(j // NB, j % NB), "head": group_of(j % NB, gain_group)},
             )
 
         return carry
@@ -183,9 +209,6 @@
         lax.fori_loop(0, TILE // ROWS, block, 0)
 
     def send_in(h, which, src_of, dst):
-        here = pltpu.make_async_copy(src_of(g * HPD + h), dst, in_recv.at[which, h])
-        here.start()
-
         def one(i, carry):
             to = (tile + i) % NH
             pltpu.make_async_remote_copy(
@@ -193,11 +216,11 @@
                 dst_ref=dst,
                 send_sem=in_send.at[which],
                 recv_sem=in_recv.at[which, h],
-                device_id={"head": to},
+                device_id={**work, "head": to},
             ).start()
             return carry
 
-        lax.fori_loop(1, NH, one, 0)
+        lax.fori_loop(0, NH, one, 0)
 
     def columns(h):
         return pl.ds(pl.multiple_of(h * HS, HS), HS)
@@ -213,72 +236,116 @@
 
     def send_g(h):
         send_in(h, 3, lambda n: g_in.at[:, columns(n)], gbuf.at[h, my_col, my_rows])
+
+    tiles = NB * 8
+    sublane = lax.broadcasted_iota(jnp.int32, (tiles, tiles), 0)
+    lane = lax.broadcasted_iota(jnp.int32, (tiles, tiles), 1)
+    live = jnp.where(sublane == lane, counts[...], 0).astype(f32)
+    live = jnp.sum(live, axis=1, keepdims=True)
+    slot = lax.broadcasted_iota(jnp.int32, (tiles, KMAX), 1).astype(f32)
+    named[...] = jnp.full((tiles, HS), NOWHERE, jnp.int32)
+    named[:, 0:KMAX] = jnp.where(slot < live, lists[...], NOWHERE)
+
+    def list_copy():
+        slab = unit(1 - d, b)[1]
+        return pltpu.make_async_remote_copy(
+            src_ref=named.at[pl.ds(pl.multiple_of(slab * 8, 8), 8)],
+            dst_ref=named_here,
+            send_sem=list_sem.at[0],
+            recv_sem=list_sem.at[1],
+            device_id=other_core,
+        )
+
+    def build_bias():
+        @pl.when(lists_local)
+        def _():
+            named_here[...] = named[pl.ds(pl.multiple_of(slab_here * 8, 8), 8), :]
+
+        @pl.when(jnp.logical_not(lists_local))
+        def _():
+            list_copy().wait_recv()
+
+        found = (named_here[...] - (slab_here - 1) * 8).astype(f32)
+        first_row = lax.broadcasted_iota(jnp.int32, (1, CH), 1) < TILE
+        for near in range(24):
+            hit = jnp.max(jnp.where(found == near, 1.0, 0.0), axis=1, keepdims=True)
+            away = jnp.broadcast_to(jnp.where(hit > 0.5, 0.0, FAR), (8, CH))
+            slab, row, col = near // 8, near // COLS % 2, near % COLS
+            for c in range(COLS):
+                bias[c * 12 + col * 3 + slab, row : row + 1, :] = jnp.where(
+                    first_row, away[c : c + 1], away[COLS + c : COLS + c + 1]
+                )
 
     normalize(k_in, k_gain, k_stage, k_fac)
     pl.semaphore_wait(
         barrier,
-        NH
-        - 1
+        2 * NH
+        + 1
         + 4 * NB
         - 2 * gain_self.astype(jnp.int32)
         + has_low.astype(jnp.int32)
         + has_high.astype(jnp.int32),
     )
+    @pl.when(lists_local)
+    def _():
+        list_copy().start()
+
     send_v(0)
     send_k(0)
+    send_g(0)
     normalize(q_in, q_gain, q_stage, q_fac)
     send_q(0)
-    send_g(0)
-
-    def halo_copy(h, which, up):
+    build_bias()
+
+    def halo_copy(h, c, which, up):
         buf = (kbuf, vbuf)[which]
         side = 0 if up else 1
         return pltpu.make_async_remote_copy(
-            src_ref=buf.at[h, :, 1],
-            dst_ref=buf.at[h, :, 0 if up else 2],
-            send_sem=halo_send.at[h, which, side],
-            recv_sem=halo_recv.at[h, which, side],
+            src_ref=buf.at[h, c, 1],
+            dst_ref=buf.at[h, c, 0 if up else 2],
+            send_sem=halo_send.at[h * COLS + c, which, side],
+            recv_sem=halo_recv.at[h * COLS + c, which, side],
             device_id=above if up else below,
         )
 
     def forward(h):
         wait_for(kbuf.at[h, :, 1], in_recv.at[0, h])
         wait_for(vbuf.at[h, :, 1], in_recv.at[1, h])
+
+        def one(c, carry):
+            for which in range(2):
+
+                @pl.when(has_high)
+                def _():
+                    halo_copy(h, c, which, True).start()
+
+                @pl.when(has_low)
+                def _():
+                    halo_copy(h, c, which, False).start()
+
+            return carry
+
+        lax.fori_loop(0, COLS, one, 0)
+
+    def await_halo(h, c):
         for which in range(2):
+
+            @pl.when(has_low)
+            def _():
+                halo_copy(h, c, which, True).wait_recv()
 
             @pl.when(has_high)
             def _():
-                halo_copy(h, which, True).start()
-
-            @pl.when(has_low)
-            def _():
-                halo_copy(h, which, False).start()
-
-    def await_halo(h):
-        for which in range(2):
-
-            @pl.when(has_low)
-            def _():
-                halo_copy(h, which, True).wait_recv()
-
-            @pl.when(has_high)
-            def _():
-                halo_copy(h, which, False).wait_recv()
+                halo_copy(h, c, which, False).wait_recv()
 
     def send_back(which, src, dst, t):
-        @pl.when(t == tile)
-        def _():
-            pltpu.make_async_copy(src, dst, back_recv.at[which]).start()
-
-        @pl.when(t != tile)
-        def _():
-            pltpu.make_async_remote_copy(
-                src_ref=src,
-                dst_ref=dst,
-                send_sem=back_send.at[which],
-                recv_sem=back_recv.at[which],
-                device_id={"head": t},
-            ).start()
+        pltpu.make_async_remote_copy(
+            src_ref=src,
+            dst_ref=dst,
+            send_sem=back_send.at[which],
+            recv_sem=back_recv.at[which],
+            device_id={"dp": seq, "blk": slab_here, "head": t},
+        ).start()
 
     def attend(h, c):
         low = jnp.maximum(c - 1, 0)
@@ -389,21 +456,14 @@
             send_back(2, own_send.at[e, 0, rows], dk_recv.at[g * HPD + h], t)
             send_back(3, own_send.at[e, 1, rows], vgrad_out.at[:, columns(g * HPD + h)], t)
 
-    def start_head(h):
-        await_halo(h)
-        wait_for(qbuf.at[h], in_recv.at[2, h])
-        wait_for(gbuf.at[h], in_recv.at[3, h])
-
-        def turn(k, carry):
-            for slab in range(3):
-                keys = slice(slab * CH, (slab + 1) * CH)
-                kt_buf[k, :, keys] = kbuf[h, k, slab].T
-                vt_buf[k, :, keys] = vbuf[h, k, slab].T
-                acc_k[k * 3 + slab] = jnp.zeros((CH, HS), f32)
-                acc_v[k * 3 + slab] = jnp.zeros((CH, HS), f32)
-            return carry
-
-        lax.fori_loop(0, COLS, turn, 0)
+    def start_column(h, k):
+        await_halo(h, k)
+        for slab in range(3):
+            keys = slice(slab * CH, (slab + 1) * CH)
+            kt_buf[k, :, keys] = kbuf[h, k, slab].T
+            vt_buf[k, :, keys] = vbuf[h, k, slab].T
+            acc_k[k * 3 + slab] = jnp.zeros((CH, HS), f32)
+            acc_v[k * 3 + slab] = jnp.zeros((CH, HS), f32)
 
     gain_tab[...] = jnp.zeros_like(gain_tab)
     forward(0)
@@ -422,11 +482,18 @@
 
         @pl.when(c == 0)
         def _():
-            start_head(h)
-
-        @pl.when((c == 1) & (h < HPD - 1))
-        def _():
-            forward(h + 1)
+            start_column(h, 0)
+
+            @pl.when(h < HPD - 1)
+            def _():
+                forward(h + 1)
+
+            wait_for(qbuf.at[h], in_recv.at[2, h])
+            wait_for(gbuf.at[h], in_recv.at[3, h])
+
+        @pl.when(c < COLS - 1)
+        def _():
+            start_column(h, c + 1)
 
         attend(h, c)
 
@@ -438,9 +505,9 @@
         def _():
             finish(h, COLS - 1)
 
-        @pl.when(s > 1)
-        def _():
-            settle(s - 2)
+        @pl.when(s >= LAG)
+        def _():
+            settle(s - LAG)
 
         return carry
 
@@ -450,14 +517,14 @@
         settle(e)
         return carry
 
-    lax.fori_loop(HPD * COLS - 2, HPD * COLS, last, 0)
+    lax.fori_loop(HPD * COLS - LAG, HPD * COLS, last, 0)
 
     for h in range(HPD):
         for row, gain in ((0, q_gain), (1, k_gain)):
             gain_tab[h, row : row + 1, :] = gain_tab[h, row : row + 1, :] / gain[:, columns(g * HPD + h)]
 
     def give(j, carry):
-        dst = gain_recv.at[d * NB + b]
+        dst = gain_recv.at[seq * NB + slab_here]
         me = gain_target_is_me(j)
 
         @pl.when(me)
@@ -525,57 +592,41 @@
     def _():
         wait_for(gain_recv.at[0], gain_sem.at[0])
 
-    sent = dq_recv.at[0 : HEADS - HPD]
     for which in range(4):
-        wait_for(sent, in_send.at[which])
-        wait_for(sent, back_send.at[which])
-
-    def drain(h, carry):
+        wait_for(dq_recv, in_send.at[which])
+        wait_for(dq_recv, back_send.at[which])
+
+    @pl.when(lists_local)
+    def _():
+        list_copy().wait_send()
+
+    def drain_edges(e, carry):
         for which in range(2):
 
             @pl.when(has_high)
             def _():
-                halo_copy(h, which, True).wait_send()
+                halo_copy(e // COLS, e % COLS, which, True).wait_send()
 
             @pl.when(has_low)
             def _():
-                halo_copy(h, which, False).wait_send()
+                halo_copy(e // COLS, e % COLS, which, False).wait_send()
+
+        @pl.when(has_high)
+        def _():
+            edge_copy(e, True).wait_send()
+
+        @pl.when(has_low)
+        def _():
+            edge_copy(e, False).wait_send()
 
         return carry
 
-    lax.fori_loop(0, HPD, drain, 0)
-
-    def drain_edges(e, carry):
-        @pl.when(has_high)
-        def _():
-            edge_copy(e, True).wait_send()
-
-        @pl.when(has_low)
-        def _():
-            edge_copy(e, False).wait_send()
-
-        return carry
-
     lax.fori_loop(0, HPD * COLS, drain_edges, 0)
-
-
-def bias_table(tile_lists, tile_counts):
-    per_slab = 2 * COLS
-    slab = lax.axis_index("blk")
-    lists = lax.dynamic_slice_in_dim(tile_lists, slab * per_slab, per_slab, 0)
-    counts = lax.dynamic_slice_in_dim(tile_counts, slab * per_slab, per_slab, 0)
-    relative = lists - (slab - 1) * per_slab
-    live = jnp.arange(KMAX)[None, :] < counts[:, None]
-    named = (relative[:, :, None] == jnp.arange(3 * per_slab)[None, None, :]) & live[:, :, None]
-    table = jnp.where(jnp.any(named, axis=1), 0.0, FAR).astype(f32)
-    table = table.reshape(2, COLS, 3, 2, COLS).transpose(1, 4, 2, 3, 0)
-    return jnp.repeat(table.reshape(COLS * 12, 2, 2), TILE, axis=2)
 
 
 def shards(
     query_input, key_input, value_input, output_grad, query_gain, key_gain, tile_lists, tile_counts
 ):
-    table = bias_table(tile_lists[0], tile_counts[0])
     vmem = pl.BlockSpec(memory_space=pltpu.VMEM)
     anywhere = pl.BlockSpec(memory_space=pl.ANY)
     token = jax.ShapeDtypeStruct((TILE, F), bf16)
@@ -584,7 +635,7 @@
         kernel,
         name="tiles",
         out_shape=(token, token, token, token, jax.ShapeDtypeStruct((8, HS), f32)),
-        in_specs=[vmem] * 7,
+        in_specs=[vmem] * 8,
         out_specs=(anywhere, vmem, vmem, anywhere, vmem),
         scratch_shapes=[
             pltpu.VMEM((HEADS, TILE, HS), bf16),
@@ -610,13 +661,17 @@
             pltpu.VMEM((HPD, COLS, CH, HS), bf16),
             pltpu.VMEM((HEADS, TILE, HS), bf16),
             pltpu.VMEM((HEADS, TILE, HS), bf16),
+            pltpu.VMEM((NB * 8, HS), jnp.int32),
+            pltpu.VMEM((8, HS), jnp.int32),
+            pltpu.VMEM((12 * COLS, 2, CH), f32),
+            pltpu.SemaphoreType.DMA((2,)),
             pltpu.VMEM((HPD, 8, HS), f32),
             pltpu.VMEM((2 * NB, HPD, 8, HS), f32),
             pltpu.SemaphoreType.DMA((2,)),
             pltpu.SemaphoreType.DMA((4,)),
             pltpu.SemaphoreType.DMA((4, HPD)),
-            pltpu.SemaphoreType.DMA((HPD, 2, 2)),
-            pltpu.SemaphoreType.DMA((HPD, 2, 2)),
+            pltpu.SemaphoreType.DMA((n, 2, 2)),
+            pltpu.SemaphoreType.DMA((n, 2, 2)),
             pltpu.SemaphoreType.DMA((n, 2)),
             pltpu.SemaphoreType.DMA((n, 2)),
             pltpu.SemaphoreType.DMA((4,)),
@@ -632,7 +687,8 @@
         output_grad[0],
         query_gain[None],
         key_gain[None],
-        table,
+        tile_lists[0],
+        tile_counts,
     )
     width = F // (2 * NB * NH)
     return (

time: 175 us -> 160 us (0.914)
  Pallas kernels: 162 us -> 148 us
    pallas_call x1, Pallas kernels: 162 us -> 148 us  [shards(): pl.pallas_call(kernel, name='tiles', out_shape=(token, token, token, toke...]
    unnamed x13 -> x11, local copies, waits for them, and re-layouts: 7.63 us -> 8.26 us
where the time goes in v4:
time: 160 us; the launch traced here: 158 us
  Pallas kernels  148 us (92%)
  local copies, waits for them, and re-layouts  9.53 us (6%)
    pallas_call x1, Pallas kernels, shards(): pl.pallas_call(kernel, name='tiles', out_shape=(token, token, token, toke...  148 us
    unnamed x11, local copies, waits for them, and re-layouts  8.26 us

profile of v4, /device:TPU:1, one launch (start us, length us, event | category | flops | bytes accessed | tf_op | source)
XLA Modules:
  0.0 158.0 jit_solution(13806267211066537977)
XLA Ops:
  0.6 1.4 copy.14
  2.0 147.8 %tiles.1 = (bf16[192,3072]{1,0:T(8,128)(2,1)}, bf16[192,3072]{1,0:T(8,128)(2,1)}, bf16[192,3072]{1,0:T(8,128)(2,1)}, bf16[192,3072]{1,0:T(8,128)(2,1)}, f32[8,128]{1,0:T(8,128)}) custom-call(bf16[192,3072]{1,0:T(8,128)(2,1)} %bitcast.15, bf16[192,3072]{1,0:T(8,128)(2,1)} %bitcast.16, bf16[192,3072]{1,0:T(8,128)(2,1)} %bitcast.17, ...), custom_call_target="tpu_custom_call" | custom-call | tf_op jit(solution)/shard_map/tiles/pallas_call | solution.py:634
  149.9 1.3 slice_bitcast_fusion
  151.1 0.0 copy-start.2
  151.1 2.5 %copy.19 = bf16[1,192,3072]{2,1,0:T(8,128)(2,1)} copy(bf16[1,192,3072]{2,1,0:T(8,128)(2,1)} %bitcast.22) | data formatting | bytes 2359296
  153.6 0.0 copy-done.2
  153.6 0.0 copy-start.1
  153.6 1.0 copy.20
  154.6 0.7 copy-done.1
  155.3 0.0 copy-start
  155.3 1.0 copy.21
  156.3 0.7 copy-done
  157.0 1.0 copy.22
Async XLA Ops:
  151.1 2.5 %copy-start.2 = (bf16[192,3072]{1,0:T(8,128)(2,1)S(1)}, bf16[192,3072]{1,0:T(8,128)(2,1)}, u32[]{:S(2)}) copy-start(bf16[192,3072]{1,0:T(8,128)(2,1)} %get-tuple-element.12) | copy-start | bytes 3538948
  153.6 1.7 %copy-start.1 = (bf16[192,3072]{1,0:T(8,128)(2,1)S(1)}, bf16[192,3072]{1,0:T(8,128)(2,1)}, u32[]{:S(2)}) copy-start(bf16[192,3072]{1,0:T(8,128)(2,1)} %get-tuple-element.13) | copy-start | bytes 3538948
  155.3 1.7 %copy-start = (bf16[192,3072]{1,0:T(8,128)(2,1)S(1)}, bf16[192,3072]{1,0:T(8,128)(2,1)}, u32[]{:S(2)}) copy-start(bf16[192,3072]{1,0:T(8,128)(2,1)} %get-tuple-element.14) | copy-start | bytes 3538948

commit v5 on v4

--- a/solution.py
+++ b/solution.py
@@ -18,12 +18,14 @@
 F = HEADS * HS
 CH = 2 * TILE
 ROWS = 16
+BLOCK = 64
+WIDTH = 24
 LAG = 3
 EPSILON = 1e-06
 SCALE = HS**-0.5
 SCALE2 = SCALE * 1.4426950408889634
 FAR = -1e30
-NOWHERE = -1000
+NOWHERE = -1000.0
 f32 = jnp.float32
 bf16 = jnp.bfloat16
 
@@ -68,14 +70,15 @@
     lists,
     counts,
     att_out,
-    qgrad_out,
-    kgrad_out,
+    dq_recv,
+    dk_recv,
     vgrad_out,
     gain_out,
+    q_tokens,
+    k_tokens,
+    token_sem,
     q_stage,
     k_stage,
-    q_fac,
-    k_fac,
     qbuf,
     gbuf,
     kbuf,
@@ -93,8 +96,7 @@
     own_send,
     o_send,
     dq_send,
-    dq_recv,
-    dk_recv,
+    slots,
     named,
     named_here,
     bias,
@@ -191,7 +193,10 @@
     def _():
         clear_side(2, 1)
 
-    def normalize(x_in, gain, stage, fac):
+    for which, (src, dst) in enumerate(((k_in, k_tokens), (q_in, q_tokens))):
+        pltpu.make_async_copy(src, dst, token_sem.at[which]).start()
+
+    def normalize(x_in, gain, stage):
         def block(i, carry):
             rows = pl.ds(pl.multiple_of(i * ROWS, ROWS), ROWS)
             total = jnp.zeros((ROWS, HS), f32)
@@ -200,7 +205,6 @@
                 total = total + x * x
             mean = jnp.sum(total, axis=1, keepdims=True) * (1.0 / F)
             factor = jnp.broadcast_to(lax.rsqrt(mean + EPSILON), (ROWS, HS))
-            fac[rows, :] = factor
             for h in range(HEADS):
                 x = x_in[rows, h * HS : (h + 1) * HS].astype(f32)
                 stage[h, rows, :] = (x * factor * gain[:, h * HS : (h + 1) * HS]).astype(bf16)
@@ -238,13 +242,10 @@
         send_in(h, 3, lambda n: g_in.at[:, columns(n)], gbuf.at[h, my_col, my_rows])
 
     tiles = NB * 8
-    sublane = lax.broadcasted_iota(jnp.int32, (tiles, tiles), 0)
-    lane = lax.broadcasted_iota(jnp.int32, (tiles, tiles), 1)
-    live = jnp.where(sublane == lane, counts[...], 0).astype(f32)
-    live = jnp.sum(live, axis=1, keepdims=True)
-    slot = lax.broadcasted_iota(jnp.int32, (tiles, KMAX), 1).astype(f32)
-    named[...] = jnp.full((tiles, HS), NOWHERE, jnp.int32)
-    named[:, 0:KMAX] = jnp.where(slot < live, lists[...], NOWHERE)
+    slot = lax.broadcasted_iota(jnp.int32, (KMAX, tiles), 0)
+    slots[...] = jnp.full((HS, HS), NOWHERE, f32)
+    slots[0:KMAX, 0:tiles] = jnp.where(slot < counts[...], lists[:, 0, :], NOWHERE).astype(f32)
+    named[...] = slots[...].T
 
     def list_copy():
         slab = unit(1 - d, b)[1]
@@ -265,7 +266,7 @@
         def _():
             list_copy().wait_recv()
 
-        found = (named_here[...] - (slab_here - 1) * 8).astype(f32)
+        found = named_here[...] - ((slab_here - 1) * 8).astype(f32)
         first_row = lax.broadcasted_iota(jnp.int32, (1, CH), 1) < TILE
         for near in range(24):
             hit = jnp.max(jnp.where(found == near, 1.0, 0.0), axis=1, keepdims=True)
@@ -276,7 +277,8 @@
                     first_row, away[c : c + 1], away[COLS + c : COLS + c + 1]
                 )
 
-    normalize(k_in, k_gain, k_stage, k_fac)
+    wait_for(k_tokens, token_sem.at[0])
+    normalize(k_tokens, k_gain, k_stage)
     pl.semaphore_wait(
         barrier,
         2 * NH
@@ -293,7 +295,8 @@
     send_v(0)
     send_k(0)
     send_g(0)
-    normalize(q_in, q_gain, q_stage, q_fac)
+    wait_for(q_tokens, token_sem.at[1])
+    normalize(q_tokens, q_gain, q_stage)
     send_q(0)
     build_bias()
 
@@ -545,30 +548,6 @@
 
     lax.fori_loop(0, 2 * NB, give, 0)
 
-    def norm_back(x_in, gain, fac, d_recv, grad_out):
-        def block(i, carry):
-            rows = pl.ds(pl.multiple_of(i * ROWS, ROWS), ROWS)
-            factor = fac[rows, :]
-            total = jnp.zeros((ROWS, HS), f32)
-            for h in range(HEADS):
-                lanes = slice(h * HS, (h + 1) * HS)
-                hat = x_in[rows, lanes].astype(f32) * factor
-                product = d_recv[h, rows, :].astype(f32) * hat
-                total = total + product * gain[:, lanes]
-            inner = jnp.sum(total, axis=1, keepdims=True) * (1.0 / F)
-            for h in range(HEADS):
-                lanes = slice(h * HS, (h + 1) * HS)
-                hat = x_in[rows, lanes].astype(f32) * factor
-                scaled = d_recv[h, rows, :].astype(f32) * gain[:, lanes]
-                grad_out[rows, lanes] = (factor * (scaled - hat * inner)).astype(bf16)
-            return carry
-
-        lax.fori_loop(0, TILE // ROWS, block, 0)
-
-    wait_for(dq_recv, back_recv.at[1])
-    norm_back(q_in, q_gain, q_fac, dq_recv, qgrad_out)
-    wait_for(dk_recv, back_recv.at[2])
-    norm_back(k_in, k_gain, k_fac, dk_recv, kgrad_out)
     wait_for(gain_recv, gain_sem.at[1])
     start = 24 * ((b % 2) * NH + tile)
     lane = lax.broadcasted_iota(jnp.int32, (HS, HS), 1)
@@ -584,6 +563,8 @@
         )
     gain_out[...] = sums
     wait_for(att_out, back_recv.at[0])
+    wait_for(dq_recv, back_recv.at[1])
+    wait_for(dk_recv, back_recv.at[2])
     wait_for(vgrad_out, back_recv.at[3])
 
     wait_for(gain_recv.at[0 : 2 * NB - 1], gain_sem.at[0])
@@ -622,6 +603,47 @@
         return carry
 
     lax.fori_loop(0, HPD * COLS, drain_edges, 0)
+
+
+def norm_back(x_in, gain, d_in, grad_out):
+    def block(i, carry):
+        rows = pl.ds(pl.multiple_of(i * ROWS, ROWS), ROWS)
+        squares = jnp.zeros((ROWS, HS), f32)
+        total = jnp.zeros((ROWS, HS), f32)
+        for h in range(HEADS):
+            lanes = slice(h * HS, (h + 1) * HS)
+            x = x_in[rows, lanes].astype(f32)
+            squares = squares + x * x
+            total = total + d_in[h, rows, :].astype(f32) * gain[:, lanes] * x
+        mean = jnp.sum(squares, axis=1, keepdims=True) * (1.0 / F)
+        factor = lax.rsqrt(mean + EPSILON)
+        inner = jnp.sum(total, axis=1, keepdims=True) * factor * (1.0 / F)
+        factor = jnp.broadcast_to(factor, (ROWS, HS))
+        inner = jnp.broadcast_to(inner, (ROWS, HS)) * factor
+        for h in range(HEADS):
+            lanes = slice(h * HS, (h + 1) * HS)
+            x = x_in[rows, lanes].astype(f32)
+            scaled = d_in[h, rows, :].astype(f32) * gain[:, lanes]
+            grad_out[rows, lanes] = (factor * (scaled - x * inner)).astype(bf16)
+        return carry
+
+    lax.fori_loop(0, BLOCK // ROWS, block, 0)
+
+
+def closing(
+    att_in, dv_in, q_in, k_in, dq_in, dk_in, q_gain, k_gain, gain_in,
+    att_out, dv_out, q_out, k_out, q_gain_out, k_gain_out,
+):
+    att_out[...] = att_in[...]
+    dv_out[...] = dv_in[...]
+
+    @pl.when(pl.program_id(0) == 0)
+    def _():
+        q_gain_out[...] = gain_in[0:1, 0:WIDTH]
+        k_gain_out[...] = gain_in[1:2, 0:WIDTH]
+
+    norm_back(q_in, q_gain, dq_in, q_out)
+    norm_back(k_in, k_gain, dk_in, k_out)
 
 
 def shards(
@@ -630,18 +652,20 @@
     vmem = pl.BlockSpec(memory_space=pltpu.VMEM)
     anywhere = pl.BlockSpec(memory_space=pl.ANY)
     token = jax.ShapeDtypeStruct((TILE, F), bf16)
+    heads = jax.ShapeDtypeStruct((HEADS, TILE, HS), bf16)
     n = HPD * COLS
-    attention, query_grad, key_grad, value_grad, gains = pl.pallas_call(
+    attention, dq, dk, value_grad, gains = pl.pallas_call(
         kernel,
         name="tiles",
-        out_shape=(token, token, token, token, jax.ShapeDtypeStruct((8, HS), f32)),
-        in_specs=[vmem] * 8,
-        out_specs=(anywhere, vmem, vmem, anywhere, vmem),
+        out_shape=(token, heads, heads, token, jax.ShapeDtypeStruct((8, HS), f32)),
+        in_specs=[anywhere] * 4 + [vmem] * 4,
+        out_specs=(anywhere,) * 4 + (vmem,),
         scratch_shapes=[
+            pltpu.VMEM((TILE, F), bf16),
+            pltpu.VMEM((TILE, F), bf16),
+            pltpu.SemaphoreType.DMA((2,)),
             pltpu.VMEM((HEADS, TILE, HS), bf16),
             pltpu.VMEM((HEADS, TILE, HS), bf16),
-            pltpu.VMEM((TILE, HS), f32),
-            pltpu.VMEM((TILE, HS), f32),
             pltpu.VMEM((HPD, COLS, CH, HS), bf16),
             pltpu.VMEM((HPD, COLS, CH, HS), bf16),
             pltpu.VMEM((HPD, COLS, 3, CH, HS), bf16),
@@ -659,10 +683,9 @@
             pltpu.VMEM((n, 2, CH, HS), bf16),
             pltpu.VMEM((HPD, COLS, CH, HS), bf16),
             pltpu.VMEM((HPD, COLS, CH, HS), bf16),
-            pltpu.VMEM((HEADS, TILE, HS), bf16),
-            pltpu.VMEM((HEADS, TILE, HS), bf16),
-            pltpu.VMEM((NB * 8, HS), jnp.int32),
-            pltpu.VMEM((8, HS), jnp.int32),
+            pltpu.VMEM((HS, HS), f32),
+            pltpu.VMEM((HS, HS), f32),
+            pltpu.VMEM((8, HS), f32),
             pltpu.VMEM((12 * COLS, 2, CH), f32),
             pltpu.SemaphoreType.DMA((2,)),
             pltpu.VMEM((HPD, 8, HS), f32),
@@ -687,17 +710,41 @@
         output_grad[0],
         query_gain[None],
         key_gain[None],
-        tile_lists[0],
+        tile_lists.transpose(2, 0, 1),
         tile_counts,
     )
-    width = F // (2 * NB * NH)
+    rows = pl.BlockSpec((BLOCK, F), lambda i: (i, 0))
+    by_head = pl.BlockSpec((HEADS, BLOCK, HS), lambda i: (0, i, 0))
+    whole = pl.BlockSpec((1, F), lambda i: (0, 0))
+    few = pl.BlockSpec((1, WIDTH), lambda i: (0, 0))
+    narrow = jax.ShapeDtypeStruct((1, WIDTH), f32)
+    attention, value_grad, query_grad, key_grad, query_gains, key_gains = pl.pallas_call(
+        closing,
+        name="closing",
+        grid=(TILE // BLOCK,),
+        out_shape=(token, token, token, token, narrow, narrow),
+        in_specs=[rows, rows, rows, rows, by_head, by_head, whole, whole]
+        + [pl.BlockSpec((8, HS), lambda i: (0, 0))],
+        out_specs=(rows, rows, rows, rows, few, few),
+        compiler_params=pltpu.CompilerParams(vmem_limit_bytes=62 * 1024 * 1024),
+    )(
+        attention,
+        value_grad,
+        query_input[0],
+        key_input[0],
+        dq,
+        dk,
+        query_gain[None],
+        key_gain[None],
+        gains,
+    )
     return (
         attention[None],
         query_grad[None],
         key_grad[None],
         value_grad[None],
-        gains[0, :width],
-        gains[1, :width],
+        query_gains[0],
+        key_gains[0],
     )
 
 

time: 160 us -> 155 us (0.969)
  local copies, waits for them, and re-layouts: 9.53 us -> 0 us
  Pallas kernels: 148 us -> 154 us
    unnamed x11 -> x0, local copies, waits for them, and re-layouts: 8.26 us -> none
    pallas_call x1 -> x2, Pallas kernels: 148 us -> 154 us  [the longest x1 146 us: shards(): pl.pallas_call(kernel, name='tiles', out_shape=(token, heads, heads, toke...]
where the time goes in v5:
time: 155 us
  Pallas kernels  154 us (99%)
    pallas_call x1, Pallas kernels, shards(): pl.pallas_call(kernel, name='tiles', out_shape=(token, heads, heads, toke...  146 us
    pallas_call x1, Pallas kernels, shards(): pl.pallas_call(closing, name='closing', grid=(TILE // BLOCK,), out_shape=...  7.57 us

profile of v5, /device:TPU:1, one launch (start us, length us, event | category | flops | bytes accessed | tf_op | source)
XLA Modules:
  0.0 154.6 jit_solution(6381791717655493936)
XLA Ops:
  0.6 146.4 %tiles.1 = (bf16[192,3072]{1,0:T(8,128)(2,1)}, bf16[24,192,128]{2,1,0:T(8,128)(2,1)}, bf16[24,192,128]{2,1,0:T(8,128)(2,1)}, bf16[192,3072]{1,0:T(8,128)(2,1)}, f32[8,128]{1,0:T(8,128)}) custom-call(bf16[192,3072]{1,0:T(8,128)(2,1)} %bitcast.13, bf16[192,3072]{1,0:T(8,128)(2,1)} %bitcast.15, bf16[192,3072]{1,0:T(8,128)(2,1)} %bitcast.17, ...), custom_call_target="tpu_custom_call" | custom-call | tf_op jit(solution)/shard_map/tiles/pallas_call | solution.py:657
  147.0 7.6 %closing.1 = (bf16[192,3072]{1,0:T(8,128)(2,1)}, bf16[192,3072]{1,0:T(8,128)(2,1)}, bf16[192,3072]{1,0:T(8,128)(2,1)}, bf16[192,3072]{1,0:T(8,128)(2,1)}, f32[1,24]{1,0:T(1,128)}, /*index=5*/f32[1,24]{1,0:T(1,128)}) custom-call(bf16[192,3072]{1,0:T(8,128)(2,1)} %get-tuple-element.17.att_in, bf16[192,3072]{1,0:T(8,128)(2,1)} %get-tuple-element.18.dv_in, ...), custom_call_target="tpu_custom_call" | custom-call | tf_op jit(solution)/shard_map/closing/pallas_call | solution.py:721

commit v6 on v5

--- a/solution.py
+++ b/solution.py
@@ -20,7 +20,7 @@
 ROWS = 16
 BLOCK = 64
 WIDTH = 24
-LAG = 3
+LAG = 5
 EPSILON = 1e-06
 SCALE = HS**-0.5
 SCALE2 = SCALE * 1.4426950408889634
@@ -125,6 +125,11 @@
     work = owner(d, b)
     lists_local = seq == d
     other_core = {"dp": 1 - d}
+    turned = g // 2 % 2
+
+    def column_at(k):
+        return k + turned * (COLS - 1 - 2 * k)
+
     my_row = tile // COLS
     my_col = tile % COLS
     gain_group = d * 4 + b // 2
@@ -315,7 +320,8 @@
         wait_for(kbuf.at[h, :, 1], in_recv.at[0, h])
         wait_for(vbuf.at[h, :, 1], in_recv.at[1, h])
 
-        def one(c, carry):
+        def one(k, carry):
+            c = column_at(k)
             for which in range(2):
 
                 @pl.when(has_high)
@@ -436,8 +442,9 @@
         def _():
             edge_copy(e, False).start()
 
-    def settle(e):
-        h, c = e // COLS, e % COLS
+    def settle(n):
+        h, c = n // COLS, column_at(n % COLS)
+        e = h * COLS + c
 
         @pl.when(has_low)
         def _():
@@ -481,11 +488,12 @@
     lax.fori_loop(1, HPD, rest, 0)
 
     def step(s, carry):
-        h, c = s // COLS, s % COLS
-
-        @pl.when(c == 0)
-        def _():
-            start_column(h, 0)
+        h, k = s // COLS, s % COLS
+        c = column_at(k)
+
+        @pl.when(k == 0)
+        def _():
+            start_column(h, c)
 
             @pl.when(h < HPD - 1)
             def _():
@@ -494,19 +502,19 @@
             wait_for(qbuf.at[h], in_recv.at[2, h])
             wait_for(gbuf.at[h], in_recv.at[3, h])
 
-        @pl.when(c < COLS - 1)
-        def _():
-            start_column(h, c + 1)
+        @pl.when(k < COLS - 1)
+        def _():
+            start_column(h, column_at(k + 1))
 
         attend(h, c)
 
-        @pl.when(c > 0)
-        def _():
-            finish(h, c - 1)
-
-        @pl.when(c == COLS - 1)
-        def _():
-            finish(h, COLS - 1)
+        @pl.when(k > 0)
+        def _():
+            finish(h, column_at(k - 1))
+
+        @pl.when(k == COLS - 1)
+        def _():
+            finish(h, c)
 
         @pl.when(s >= LAG)
         def _():

time: 155 us -> 150 us (0.968); the launches traced: 155 us -> 147 us
  Pallas kernels: 154 us -> 147 us
    pallas_call x1, Pallas kernels: 146 us -> 139 us  [shards(): pl.pallas_call(kernel, name='tiles', out_shape=(token, heads, heads, toke...]
where the time goes in v6:
time: 150 us; the launch traced here: 147 us
  Pallas kernels  147 us (98%)
    pallas_call x1, Pallas kernels, shards(): pl.pallas_call(kernel, name='tiles', out_shape=(token, heads, heads, toke...  139 us
    pallas_call x1, Pallas kernels, shards(): pl.pallas_call(closing, name='closing', grid=(TILE // BLOCK,), out_shape=...  7.57 us

profile of v6, /device:TPU:1, one launch (start us, length us, event | category | flops | bytes accessed | tf_op | source)
XLA Modules:
  0.0 147.4 jit_solution(16684000798766235315)
XLA Ops:
  0.6 139.2 %tiles.1 = (bf16[192,3072]{1,0:T(8,128)(2,1)}, bf16[24,192,128]{2,1,0:T(8,128)(2,1)}, bf16[24,192,128]{2,1,0:T(8,128)(2,1)}, bf16[192,3072]{1,0:T(8,128)(2,1)}, f32[8,128]{1,0:T(8,128)}) custom-call(bf16[192,3072]{1,0:T(8,128)(2,1)} %bitcast.13, bf16[192,3072]{1,0:T(8,128)(2,1)} %bitcast.15, bf16[192,3072]{1,0:T(8,128)(2,1)} %bitcast.17, ...), custom_call_target="tpu_custom_call" | custom-call | tf_op jit(solution)/shard_map/tiles/pallas_call | solution.py:665
  139.9 7.6 %closing.1 = (bf16[192,3072]{1,0:T(8,128)(2,1)}, bf16[192,3072]{1,0:T(8,128)(2,1)}, bf16[192,3072]{1,0:T(8,128)(2,1)}, bf16[192,3072]{1,0:T(8,128)(2,1)}, f32[1,24]{1,0:T(1,128)}, /*index=5*/f32[1,24]{1,0:T(1,128)}) custom-call(bf16[192,3072]{1,0:T(8,128)(2,1)} %get-tuple-element.17.att_in, bf16[192,3072]{1,0:T(8,128)(2,1)} %get-tuple-element.18.dv_in, ...), custom_call_target="tpu_custom_call" | custom-call | tf_op jit(solution)/shard_map/closing/pallas_call | solution.py:729

commit v7 on v6

--- a/solution.py
+++ b/solution.py
@@ -60,6 +60,31 @@
     pltpu.make_async_copy(ref, ref, sem).wait()
 
 
+def norm_back(x_in, gain, d_in, grad_out, count):
+    def block(i, carry):
+        rows = pl.ds(pl.multiple_of(i * ROWS, ROWS), ROWS)
+        squares = jnp.zeros((ROWS, HS), f32)
+        total = jnp.zeros((ROWS, HS), f32)
+        for h in range(HEADS):
+            lanes = slice(h * HS, (h + 1) * HS)
+            x = x_in[rows, lanes].astype(f32)
+            squares = squares + x * x
+            total = total + d_in[h, rows, :].astype(f32) * gain[:, lanes] * x
+        mean = jnp.sum(squares, axis=1, keepdims=True) * (1.0 / F)
+        factor = lax.rsqrt(mean + EPSILON)
+        inner = jnp.sum(total, axis=1, keepdims=True) * factor * (1.0 / F)
+        factor = jnp.broadcast_to(factor, (ROWS, HS))
+        inner = jnp.broadcast_to(inner, (ROWS, HS)) * factor
+        for h in range(HEADS):
+            lanes = slice(h * HS, (h + 1) * HS)
+            x = x_in[rows, lanes].astype(f32)
+            scaled = d_in[h, rows, :].astype(f32) * gain[:, lanes]
+            grad_out[rows, lanes] = (factor * (scaled - x * inner)).astype(bf16)
+        return carry
+
+    lax.fori_loop(0, count // ROWS, block, 0)
+
+
 def kernel(
     q_in,
     k_in,
@@ -70,7 +95,7 @@
     lists,
     counts,
     att_out,
-    dq_recv,
+    qgrad_out,
     dk_recv,
     vgrad_out,
     gain_out,
@@ -96,6 +121,7 @@
     own_send,
     o_send,
     dq_send,
+    dq_recv,
     slots,
     named,
     named_here,
@@ -556,6 +582,11 @@
 
     lax.fori_loop(0, 2 * NB, give, 0)
 
+    wait_for(dq_recv, back_recv.at[1])
+    norm_back(q_tokens, q_gain, dq_recv, k_tokens, TILE)
+    written = pltpu.make_async_copy(k_tokens, qgrad_out, token_sem.at[0])
+    written.start()
+
     wait_for(gain_recv, gain_sem.at[1])
     start = 24 * ((b % 2) * NH + tile)
     lane = lax.broadcasted_iota(jnp.int32, (HS, HS), 1)
@@ -571,9 +602,9 @@
         )
     gain_out[...] = sums
     wait_for(att_out, back_recv.at[0])
-    wait_for(dq_recv, back_recv.at[1])
     wait_for(dk_recv, back_recv.at[2])
     wait_for(vgrad_out, back_recv.at[3])
+    written.wait()
 
     wait_for(gain_recv.at[0 : 2 * NB - 1], gain_sem.at[0])
 
@@ -613,45 +644,20 @@
     lax.fori_loop(0, HPD * COLS, drain_edges, 0)
 
 
-def norm_back(x_in, gain, d_in, grad_out):
-    def block(i, carry):
-        rows = pl.ds(pl.multiple_of(i * ROWS, ROWS), ROWS)
-        squares = jnp.zeros((ROWS, HS), f32)
-        total = jnp.zeros((ROWS, HS), f32)
-        for h in range(HEADS):
-            lanes = slice(h * HS, (h + 1) * HS)
-            x = x_in[rows, lanes].astype(f32)
-            squares = squares + x * x
-            total = total + d_in[h, rows, :].astype(f32) * gain[:, lanes] * x
-        mean = jnp.sum(squares, axis=1, keepdims=True) * (1.0 / F)
-        factor = lax.rsqrt(mean + EPSILON)
-        inner = jnp.sum(total, axis=1, keepdims=True) * factor * (1.0 / F)
-        factor = jnp.broadcast_to(factor, (ROWS, HS))
-        inner = jnp.broadcast_to(inner, (ROWS, HS)) * factor
-        for h in range(HEADS):
-            lanes = slice(h * HS, (h + 1) * HS)
-            x = x_in[rows, lanes].astype(f32)
-            scaled = d_in[h, rows, :].astype(f32) * gain[:, lanes]
-            grad_out[rows, lanes] = (factor * (scaled - x * inner)).astype(bf16)
-        return carry
-
-    lax.fori_loop(0, BLOCK // ROWS, block, 0)
-
-
 def closing(
-    att_in, dv_in, q_in, k_in, dq_in, dk_in, q_gain, k_gain, gain_in,
+    att_in, dv_in, q_in, k_in, dk_in, k_gain, gain_in,
     att_out, dv_out, q_out, k_out, q_gain_out, k_gain_out,
 ):
     att_out[...] = att_in[...]
     dv_out[...] = dv_in[...]
+    q_out[...] = q_in[...]
 
     @pl.when(pl.program_id(0) == 0)
     def _():
         q_gain_out[...] = gain_in[0:1, 0:WIDTH]
         k_gain_out[...] = gain_in[1:2, 0:WIDTH]
 
-    norm_back(q_in, q_gain, dq_in, q_out)
-    norm_back(k_in, k_gain, dk_in, k_out)
+    norm_back(k_in, k_gain, dk_in, k_out, BLOCK)
 
 
 def shards(
@@ -662,10 +668,10 @@
     token = jax.ShapeDtypeStruct((TILE, F), bf16)
     heads = jax.ShapeDtypeStruct((HEADS, TILE, HS), bf16)
     n = HPD * COLS
-    attention, dq, dk, value_grad, gains = pl.pallas_call(
+    attention, query_grad, dk, value_grad, gains = pl.pallas_call(
         kernel,
         name="tiles",
-        out_shape=(token, heads, heads, token, jax.ShapeDtypeStruct((8, HS), f32)),
+        out_shape=(token, token, heads, token, jax.ShapeDtypeStruct((8, HS), f32)),
         in_specs=[anywhere] * 4 + [vmem] * 4,
         out_specs=(anywhere,) * 4 + (vmem,),
         scratch_shapes=[
@@ -691,6 +697,7 @@
             pltpu.VMEM((n, 2, CH, HS), bf16),
             pltpu.VMEM((HPD, COLS, CH, HS), bf16),
             pltpu.VMEM((HPD, COLS, CH, HS), bf16),
+            pltpu.VMEM((HEADS, TILE, HS), bf16),
             pltpu.VMEM((HS, HS), f32),
             pltpu.VMEM((HS, HS), f32),
             pltpu.VMEM((8, HS), f32),
@@ -731,18 +738,16 @@
         name="closing",
         grid=(TILE // BLOCK,),
         out_shape=(token, token, token, token, narrow, narrow),
-        in_specs=[rows, rows, rows, rows, by_head, by_head, whole, whole]
+        in_specs=[rows, rows, rows, rows, by_head, whole]
         + [pl.BlockSpec((8, HS), lambda i: (0, 0))],
         out_specs=(rows, rows, rows, rows, few, few),
         compiler_params=pltpu.CompilerParams(vmem_limit_bytes=62 * 1024 * 1024),
     )(
         attention,
         value_grad,
-        query_input[0],
+        query_grad,
         key_input[0],
-        dq,
         dk,
-        query_gain[None],
         key_gain[None],
         gains,
     )

time: 150 us -> 149 us (level)
  no operation moved by 1% of the time
where the time goes in v7:
time: 149 us; the launch traced here: 147 us
  Pallas kernels  146 us (98%)
    pallas_call x1, Pallas kernels, shards(): pl.pallas_call(kernel, name='tiles', out_shape=(token, token, heads, toke...  139 us
    pallas_call x1, Pallas kernels, shards(): pl.pallas_call(closing, name='closing', grid=(TILE // BLOCK,), out_shape=...  6.68 us

profile of v7, /device:TPU:1, one launch (start us, length us, event | category | flops | bytes accessed | tf_op | source)
XLA Modules:
  0.0 146.6 jit_solution(8836719844277265170)
XLA Ops:
  0.6 139.3 %tiles.1 = (bf16[192,3072]{1,0:T(8,128)(2,1)}, bf16[192,3072]{1,0:T(8,128)(2,1)}, bf16[24,192,128]{2,1,0:T(8,128)(2,1)}, bf16[192,3072]{1,0:T(8,128)(2,1)}, f32[8,128]{1,0:T(8,128)}) custom-call(bf16[192,3072]{1,0:T(8,128)(2,1)} %bitcast.15, bf16[192,3072]{1,0:T(8,128)(2,1)} %bitcast.13, bf16[192,3072]{1,0:T(8,128)(2,1)} %bitcast.16, ...), custom_call_target="tpu_custom_call" | custom-call | tf_op jit(solution)/shard_map/tiles/pallas_call | solution.py:671
  139.9 6.7 %closing.1 = (bf16[192,3072]{1,0:T(8,128)(2,1)}, bf16[192,3072]{1,0:T(8,128)(2,1)}, bf16[192,3072]{1,0:T(8,128)(2,1)}, bf16[192,3072]{1,0:T(8,128)(2,1)}, f32[1,24]{1,0:T(1,128)}, /*index=5*/f32[1,24]{1,0:T(1,128)}) custom-call(bf16[192,3072]{1,0:T(8,128)(2,1)} %get-tuple-element.17.att_in, bf16[192,3072]{1,0:T(8,128)(2,1)} %get-tuple-element.18.dv_in, ...), custom_call_target="tpu_custom_call" | custom-call | tf_op jit(solution)/shard_map/closing/pallas_call | solution.py:736

commit v8 on v7

--- a/solution.py
+++ b/solution.py
@@ -520,11 +520,6 @@
         @pl.when(k == 0)
         def _():
             start_column(h, c)
-
-            @pl.when(h < HPD - 1)
-            def _():
-                forward(h + 1)
-
             wait_for(qbuf.at[h], in_recv.at[2, h])
             wait_for(gbuf.at[h], in_recv.at[3, h])
 
@@ -532,6 +527,10 @@
         def _():
             start_column(h, column_at(k + 1))
 
+        @pl.when((k == 1) & (h < HPD - 1))
+        def _():
+            forward(h + 1)
+
         attend(h, c)
 
         @pl.when(k > 0)
@@ -542,9 +541,13 @@
         def _():
             finish(h, c)
 
-        @pl.when(s >= LAG)
+        @pl.when((s >= LAG) & (s < HPD * COLS - 1))
         def _():
             settle(s - LAG)
+
+        @pl.when(s >= HPD * COLS - 2)
+        def _():
+            settle(s - LAG + 1)
 
         return carry
 
@@ -554,7 +557,7 @@
         settle(e)
         return carry
 
-    lax.fori_loop(HPD * COLS - LAG, HPD * COLS, last, 0)
+    lax.fori_loop(HPD * COLS - LAG + 1, HPD * COLS, last, 0)
 
     for h in range(HPD):
         for row, gain in ((0, q_gain), (1, k_gain)):

time: 149 us -> 150 us (level)
  the two profiles are of different devices: /device:TPU:1 before, /device:TPU:31 now
where the time goes in v8:
time: 150 us
  Pallas kernels  149 us (99%)
    pallas_call x1, Pallas kernels, shards(): pl.pallas_call(kernel, name='tiles', out_shape=(token, token, heads, toke...  142 us
    pallas_call x1, Pallas kernels, shards(): pl.pallas_call(closing, name='closing', grid=(TILE // BLOCK,), out_shape=...  6.68 us

profile of v8, /device:TPU:31, one launch (start us, length us, event | category | flops | bytes accessed | tf_op | source)
XLA Modules:
  0.0 149.8 jit_solution(8145853851753000730)
XLA Ops:
  0.6 142.5 %tiles.1 = (bf16[192,3072]{1,0:T(8,128)(2,1)}, bf16[192,3072]{1,0:T(8,128)(2,1)}, bf16[24,192,128]{2,1,0:T(8,128)(2,1)}, bf16[192,3072]{1,0:T(8,128)(2,1)}, f32[8,128]{1,0:T(8,128)}) custom-call(bf16[192,3072]{1,0:T(8,128)(2,1)} %bitcast.15, bf16[192,3072]{1,0:T(8,128)(2,1)} %bitcast.13, bf16[192,3072]{1,0:T(8,128)(2,1)} %bitcast.16, ...), custom_call_target="tpu_custom_call" | custom-call | tf_op jit(solution)/shard_map/tiles/pallas_call | solution.py:674
  143.1 6.7 %closing.1 = (bf16[192,3072]{1,0:T(8,128)(2,1)}, bf16[192,3072]{1,0:T(8,128)(2,1)}, bf16[192,3072]{1,0:T(8,128)(2,1)}, bf16[192,3072]{1,0:T(8,128)(2,1)}, f32[1,24]{1,0:T(1,128)}, /*index=5*/f32[1,24]{1,0:T(1,128)}) custom-call(bf16[192,3072]{1,0:T(8,128)(2,1)} %get-tuple-element.17.att_in, bf16[192,3072]{1,0:T(8,128)(2,1)} %get-tuple-element.18.dv_in, ...), custom_call_target="tpu_custom_call" | custom-call | tf_op jit(solution)/shard_map/closing/pallas_call | solution.py:739
